TPU v7x, 128 devices: a whole 4x4x4 slice. The times are simulated.
128 devices in a mesh: ctx: 16 (over x_lo, z, core), tp: 8 (over x_hi, y).
Axes of the slice: x: 4 (x_hi: 2, x_lo: 2; x = x_hi * 2 + x_lo), y: 4, z: 4, core: 2. Of those that a mesh axis runs over, the one named last changes fastest.
Arguments:
- fine_x: bfloat16 [16384, 8192], P(('ctx', 'tp')), may hold values from -6 to 6
- fine_q: bfloat16 [16384, 8192], P(('ctx', 'tp'))
- fine_k: bfloat16 [16384, 1024], P(('ctx', 'tp'))
- fine_v: bfloat16 [16384, 1024], P(('ctx', 'tp')), may hold values from -6 to 6
- windows: int32 [64], replicated, may hold values from 128 to 512, as said below
- pool_w: float32 [4, 8192], replicated, may hold values from -3 to 3
- norm_gain: float32 [8192], replicated, may hold values from 0.5 to 2
- w_query: bfloat16 [8192, 4096], P('ctx', 'tp')
- w_key: bfloat16 [8192, 1024], P('ctx', 'tp')
- w_value: bfloat16 [8192, 1024], P('ctx', 'tp'), may hold values from -0.0625 to 0.0625
- w_out: bfloat16 [4096, 8192], P('tp', 'ctx'), may hold values from -0.09375 to 0.09375
- up_w: float32 [4, 8192], replicated, may hold values from -3 to 3
Outputs:
- fine_out: float32 [16384, 8192], P(('ctx', 'tp'))
Inputs may be any that keep to these rules, and one draw needn't show every extreme that they name: `windows`: one head's window is exactly 512.
All inputs are finite; a program needn't handle non-finite values.
Results may differ from a plain program's by a relative error of at most 0.011.
Values may be sent and summed in bfloat16 or wider, within the bound.
A program may use at most 128 MiB of HBM per device.

v0:
```python
import jax
import jax.numpy as jnp
from jax import lax
from jax.sharding import PartitionSpec as P

HEAD = 128
WIN = 512
POOL = 4


def passed_along(block, axis, distance):
    devices = range(lax.axis_size(axis))
    route = [(i - distance, i) for i in devices if i - distance in devices]
    return lax.ppermute(block, axis, route)


def attend_window(queries, key_rows, value_rows, query_pos, key_pos, windows):
    kv_heads = queries.shape[1]
    group_size = queries.shape[2]
    scores = jnp.einsum(
        "qkgd,lkd->kgql", queries, key_rows, preferred_element_type=jnp.float32
    ) * HEAD ** (-0.5)
    distance = query_pos[:, None] - key_pos[None, :]
    spans = windows.reshape(kv_heads, group_size, 1, 1)
    allowed = (
        (distance[None, None] >= 0)
        & (distance[None, None] < spans)
        & (key_pos[None, None, None, :] >= 0)
    )
    scores = jnp.where(allowed, scores, -1e30)
    row_top = scores.max(-1, keepdims=True)
    weights = jnp.where(allowed, jnp.exp(scores - row_top), 0.0)
    row_total = weights.sum(-1)
    mixed_heads = jnp.einsum(
        "kgql,lkd->qkgd",
        weights.astype(jnp.bfloat16),
        value_rows,
        preferred_element_type=jnp.float32,
    )
    return mixed_heads / jnp.transpose(row_total, (2, 0, 1))[..., None]


def per_device(
    fine_x, fine_q, fine_k, fine_v, windows, pool_w, norm_gain, w_query, w_key, w_value, w_out, up_w
):
    tok_rows = fine_x.shape[0]
    model_width = fine_x.shape[1]
    kv_width = fine_k.shape[1]
    kv_heads = kv_width // HEAD
    group_size = fine_q.shape[1] // kv_width
    reach_blocks = (WIN + tok_rows - 2) // tok_rows
    stacked = jnp.stack((fine_k, fine_v))
    earlier = [
        passed_along(stacked, ("ctx", "tp"), reach_blocks - offset)
        for offset in range(reach_blocks)
    ]
    joined = jnp.concatenate(earlier + [stacked], axis=1)
    device_pos = lax.axis_index(("ctx", "tp"))
    query_pos = device_pos * tok_rows + jnp.arange(tok_rows, dtype=jnp.int32)
    key_pos = (
        device_pos * tok_rows
        - reach_blocks * tok_rows
        + jnp.arange((reach_blocks + 1) * tok_rows, dtype=jnp.int32)
    )
    span_rows = joined.shape[1]
    attended = attend_window(
        fine_q.reshape(tok_rows, kv_heads, group_size, HEAD),
        joined[0].reshape(span_rows, kv_heads, HEAD),
        joined[1].reshape(span_rows, kv_heads, HEAD),
        query_pos,
        key_pos,
        windows,
    ).reshape(tok_rows, model_width)
    stream = fine_x.astype(jnp.float32) + attended
    pool_rows = tok_rows // POOL
    pooled = (stream.reshape(pool_rows, POOL, model_width) * pool_w[None]).sum(1)
    block_f = lax.all_gather(pooled, "tp", axis=0, tiled=True)
    normed = (
        block_f
        * lax.rsqrt(jnp.mean(block_f * block_f, -1, keepdims=True) + 1e-05)
        * norm_gain[None]
    ).astype(jnp.bfloat16)
    coarse_rows = block_f.shape[0]
    query_full, key_full, value_full = (
        lax.all_gather(w_query, "ctx", axis=0, tiled=True),
        lax.all_gather(w_key, "ctx", axis=0, tiled=True),
        lax.all_gather(w_value, "ctx", axis=0, tiled=True),
    )
    query_proj = jnp.dot(normed, query_full, preferred_element_type=jnp.float32)
    key_proj = jnp.dot(normed, key_full, preferred_element_type=jnp.float32)
    value_proj = jnp.dot(normed, value_full, preferred_element_type=jnp.float32)
    queries = query_proj.astype(jnp.bfloat16)
    key_rows = key_proj.astype(jnp.bfloat16)
    value_rows = value_proj.astype(jnp.bfloat16)
    local_kv = key_rows.shape[1] // HEAD
    query_group = queries.shape[1] // key_rows.shape[1]
    query_heads = queries.reshape(coarse_rows, local_kv, query_group, HEAD)
    coarse_pos = lax.axis_index("ctx") * coarse_rows + jnp.arange(coarse_rows, dtype=jnp.int32)
    row_top = jnp.full((local_kv, query_group, coarse_rows), -1e30, jnp.float32)
    key_piece = lax.all_gather(key_rows, "ctx", axis=0, tiled=True)
    value_piece = lax.all_gather(value_rows, "ctx", axis=0, tiled=True)
    span_now = key_piece.shape[0]
    piece_pos = jnp.arange(span_now, dtype=jnp.int32)
    scores = jnp.einsum(
        "qkgd,lkd->kgql",
        query_heads,
        key_piece.reshape(span_now, local_kv, HEAD),
        preferred_element_type=jnp.float32,
    ) * HEAD ** (-0.5)
    allowed = piece_pos[None, :] <= coarse_pos[:, None]
    scores = jnp.where(allowed[None, None], scores, -1e30)
    new_top = jnp.maximum(row_top, scores.max(-1))
    weights = jnp.where(allowed[None, None], jnp.exp(scores - new_top[..., None]), 0.0)
    row_total = weights.sum(-1)
    update = jnp.einsum(
        "kgql,lkd->qkgd",
        weights.astype(jnp.bfloat16),
        value_piece.reshape(span_now, local_kv, HEAD),
        preferred_element_type=jnp.float32,
    )
    accum = update
    row_top, row_total, accum = (new_top, row_total, accum)
    head_out = (
        (accum / jnp.transpose(row_total, (2, 0, 1))[..., None])
        .reshape(coarse_rows, local_kv * query_group * HEAD)
        .astype(jnp.bfloat16)
    )
    out_full = lax.all_gather(w_out, "ctx", axis=1, tiled=True)
    attn_rows = lax.psum_scatter(
        jnp.dot(head_out, out_full, preferred_element_type=jnp.float32).astype(jnp.bfloat16),
        "tp",
        scatter_dimension=0,
        tiled=True,
    ).astype(jnp.float32)
    coarse = pooled + attn_rows
    last_row = passed_along(coarse[-1:].astype(jnp.bfloat16), ("ctx", "tp"), 1).astype(jnp.float32)
    shifted = jnp.concatenate([last_row, coarse[:-1]], 0)
    result = stream.reshape(pool_rows, POOL, model_width) + up_w[None] * shifted[:, None, :]
    return result.reshape(tok_rows, model_width)


def solution(mesh):
    placed = (
        P(("ctx", "tp"), None),
        P(("ctx", "tp"), None),
        P(("ctx", "tp"), None),
        P(("ctx", "tp"), None),
        P(),
        P(),
        P(),
        P("ctx", "tp"),
        P("ctx", "tp"),
        P("ctx", "tp"),
        P("tp", "ctx"),
        P(),
    )
    return jax.shard_map(
        per_device, mesh=mesh, in_specs=placed, out_specs=P(("ctx", "tp"), None), check_vma=False
    )
```

profile of v0, /device:TPU:0, one launch (start us, length us, event | category | flops | bytes accessed | tf_op | source)
XLA Modules:
  0.0 590.3 jit_solution(16976237236086313131)
XLA Ops:
  6.5 1.1 copy.20
  7.7 1.1 copy.19
  8.8 5.8 collective-permute-start
  14.7 5.7 collective-permute-start.1
  20.4 2.3 collective-permute-start.2
  22.7 3.2 collective-permute-start.3
  26.2 1.3 lt.16
  27.6 2.2 copy.34
  30.3 1.1 constant_dynamic-update-slice_fusion.4
  31.4 2.1 collective-permute-done.1
  33.5 1.2 constant_dynamic-update-slice_fusion.3
  34.7 1.2 constant_dynamic-update-slice_fusion.2
  35.8 9.2 %collective-permute-done.3 = bf16[2,128,1024]{1,2,0:T(8,128)(2,1)} collective-permute-done((bf16[2,128,1024]{1,2,0:T(8,128)(2,1)S(1)}, bf16[2,128,1024]{1,2,0:T(8,128)(2,1)}, u32[]{:S(2)}, u32[]{:S(2)}) %collective-permute-start.3) | collective-permute-done | bytes 524320 | tf_op jit(solution)/shard_map/ppermute | solution.py:14
  45.1 1.2 constant_dynamic-update-slice_fusion.1
  46.4 1.7 fusion.45
  48.1 19.7 %fusion.46 = (f32[8,8,128]{2,1,0:T(8,128)S(1)}, bf16[8,8,128,640]{2,3,1,0:T(8,128)(2,1)}) fusion(s32[8,8]{1,0:T(8,128)} %lt.16, s32[128,640]{0,1:T(8,128)S(1)} %broadcast_subtract_fusion, pred[640]{0:T(1024)(128)(4,1)} %broadcast_compare_fusion.1, pred[128,640]{0,1:T(8,128)(4,1)S(1)} %broadcast_compare_fusion, bf16[640,8,128,1]{0,2,3,1:T(8,128)(2,1)} %bitcast.110, ...), kind=kOutput, calls=%fused_computation.60 | convolution fusion | flops 1405092480 | bytes 14336896 | tf_op jit(solution)/shard_map/sub | solution.py:32
  67.8 8.2 %bitcast_divide_fusion = f32[128,8,8,128]{0,3,2,1:T(8,128)} fusion(bf16[640,8,128,1]{0,2,3,1:T(8,128)(2,1)} %bitcast.109, bf16[8,8,128,640]{2,3,1,0:T(8,128)(2,1)} %get-tuple-element.8, f32[128,8,8]{0,2,1:T(8,128)S(1)} %bitcast.113), kind=kOutput, calls=%fused_computation.18 | convolution fusion | flops 1343225856 | bytes 16023552 | tf_op jit(solution)/shard_map/kgql,lkd->qkgd/dot_general | solution.py:34
  76.0 5.8 copy.24
  81.8 4.6 convert_add_fusion
  86.4 5.2 reshape.159
  91.6 6.0 %multiply_reduce_fusion.1 = f32[32,8192]{1,0:T(8,128)} fusion(f32[32,4,8192]{2,1,0:T(4,128)} %reshape.159, f32[4,8192]{1,0:T(4,128)S(1)} %copy-done.4), kind=kLoop, calls=%fused_computation.20 | loop fusion | flops 1835008 | bytes 5373952 | tf_op jit(solution)/shard_map/reduce_sum | solution.py:76
  97.8 0.7 all-gather.14.cloned.1.call-update
  99.8 122.1 %all-gather.8.cloned.1.call-done = f32[256,8192]{1,0:T(8,128)} async-done(((f32[32,8192]{1,0:T(8,128)}), f32[256,8192]{1,0:T(8,128)}) %all-gather.8.cloned.1.call-update) | async-done | bytes 8388624 | tf_op jit(solution)/shard_map/all_gather | solution.py:77
  221.9 4.2 multiply_reduce_fusion
  226.1 1.6 copy-done
  227.7 3.1 multiply_convert_fusion
  230.8 25.0 %all-gather.14.cloned.1.call-done = bf16[8192,128]{1,0:T(8,128)(2,1)} async-done(((bf16[512,128]{1,0:T(8,128)(2,1)}), bf16[8192,128]{1,0:T(8,128)(2,1)}) %all-gather.14.cloned.1.call-update) | async-done | bytes 2097168 | tf_op jit(solution)/shard_map/all_gather | solution.py:86
  255.8 4.7 convolution_convert_fusion.2
  260.6 30.9 %all-gather.10.cloned.1.call-done = bf16[8192,128]{1,0:T(8,128)(2,1)} async-done(((bf16[512,128]{1,0:T(8,128)(2,1)}), bf16[8192,128]{1,0:T(8,128)(2,1)}) %all-gather.10.cloned.1.call-update) | async-done | bytes 2097168 | tf_op jit(solution)/shard_map/all_gather | solution.py:87
  291.5 5.0 convolution_convert_fusion.3
  296.6 0.7 all-gather.20.cloned.1.call-update
  298.1 47.0 %all-gather.18.cloned.1.call-done = bf16[8192,512]{1,0:T(8,128)(2,1)} async-done(((bf16[512,512]{1,0:T(8,128)(2,1)}), bf16[8192,512]{1,0:T(8,128)(2,1)}) %all-gather.18.cloned.1.call-update) | async-done | bytes 8388624 | tf_op jit(solution)/shard_map/all_gather | solution.py:85
  345.1 7.0 %fusion.22 = bf16[32,4,8,128]{3,2,1,0:T(8,128)(2,1)S(1)} fusion(bf16[256,8192]{1,0:T(8,128)(2,1)} %multiply_convert_fusion, bf16[8192,512]{1,0:T(8,128)(2,1)} %all-gather.18.cloned.1.call-done), kind=kOutput, calls=%fused_computation.27 | convolution fusion | flops 2147614720 | bytes 12845056 | tf_op jit(solution)/shard_map/dot_general | solution.py:89
  352.1 28.1 %all-gather.16.cloned.1.call-done = bf16[4096,128]{1,0:T(8,128)(2,1)} async-done(((bf16[256,128]{1,0:T(8,128)(2,1)}), bf16[4096,128]{1,0:T(8,128)(2,1)}) %all-gather.16.cloned.1.call-update) | async-done | bytes 1048592 | tf_op jit(solution)/shard_map/all_gather | solution.py:100
  380.2 4.0 fusion.1
  384.2 5.7 copy-done.1
  389.9 4.2 fusion.2
  394.1 21.7 %all-gather.12.cloned.1.call-done = bf16[4096,128]{0,1:T(8,128)(2,1)} async-done(((bf16[256,128]{0,1:T(8,128)(2,1)}), bf16[4096,128]{0,1:T(8,128)(2,1)}) %all-gather.12.cloned.1.call-update) | async-done | bytes 1048592 | tf_op jit(solution)/shard_map/all_gather | solution.py:101
  415.8 10.4 %fusion.31 = bf16[256,1,4,128]{0,3,2,1:T(8,128)(2,1)S(1)} fusion(f32[4096,256,4]{1,0,2:T(8,128)} %copy-done.1, f32[4,256]{1,0:T(4,128)S(1)} %broadcast_maximum_fusion, pred[256,4096]{0,1:T(8,128)(4,1)S(1)} %iota_compare_fusion, bf16[4096,128]{0,1:T(8,128)(2,1)} %all-gather.12.cloned.1.call-done, f32[256,4]{0,1:T(4,128)S(1)} %bitcast.112), kind=kOutput, calls=%fused_computation.36 | convolution fusion | flops 1094975488 | bytes 19144704 | tf_op jit(solution)/shard_map/kgql,lkd->qkgd/dot_general | solution.py:115
  426.2 43.5 %all-gather.20.cloned.1.call-done = bf16[512,8192]{1,0:T(8,128)(2,1)} async-done(((bf16[512,512]{1,0:T(8,128)(2,1)}), bf16[512,8192]{1,0:T(8,128)(2,1)}) %all-gather.20.cloned.1.call-update) | async-done | bytes 8388624 | tf_op jit(solution)/shard_map/all_gather | solution.py:128
  469.7 7.7 %convolution_convert_fusion = bf16[256,8192]{1,0:T(8,128)(2,1)} fusion(bf16[256,512]{0,1:T(8,128)(2,1)S(1)} %bitcast.111, bf16[512,8192]{1,0:T(8,128)(2,1)} %all-gather.20.cloned.1.call-done), kind=kOutput, calls=%fused_computation.11 | convolution fusion | flops 2149580800 | bytes 12845056 | tf_op jit(solution)/shard_map/dot_general | solution.py:130
  477.4 85.5 %reduce-scatter.2.cloned.1.call-done = bf16[32,8192]{1,0:T(8,128)(2,1)} async-done(((bf16[256,8192]{1,0:T(8,128)(2,1)}), bf16[32,8192]{1,0:T(8,128)(2,1)}) %reduce-scatter.2.cloned.1.call-update) | async-done | bytes 524304 | tf_op jit(solution)/shard_map/reduce_scatter | solution.py:129
  563.0 1.1 convert_add_fusion.1
  564.1 3.1 collective-permute-start.4
  567.3 1.6 collective-permute-done.4
  569.0 3.1 broadcast_multiply_fusion
  572.1 5.3 mul.95
  577.5 6.0 %add.72 = f32[128,8192]{1,0:T(8,128)} add(f32[128,8192]{1,0:T(8,128)} %convert_add_fusion, f32[128,8192]{1,0:T(8,128)} %mul.95) | non-fusion elementwise | flops 1048576 | bytes 12582912 | tf_op jit(solution)/shard_map/add | solution.py:138
  (42 shorter events, 3.5 us)
Async XLA Ops:
  6.5 215.4 %all-gather.8.cloned.1.call-start = ((), (), s32[]{:S(2)}) async-start(), calls=%async_computation.1 | async-start | bytes 9437184 | tf_op jit(solution)/shard_map/all_gather | solution.py:77
  8.8 21.5 %collective-permute-start = (bf16[2,128,1024]{1,2,0:T(8,128)(2,1)S(1)}, bf16[2,128,1024]{1,2,0:T(8,128)(2,1)}, u32[]{:S(2)}, u32[]{:S(2)}) collective-permute-start(bf16[2,128,1024]{1,2,0:T(8,128)(2,1)S(1)} %pad_maximum_fusion.1), channel_id=1, source_target_pairs={{0,4},{1,5},{2,6},{3,7},{4,8},{5,9},{6,10},{7,11},{8,12},{9,13},{1... | collective-permute-start | bytes 1572872 | tf_op jit(solution)/shard_map/ppermute | solution.py:14
  14.7 18.8 %collective-permute-start.1 = (bf16[2,128,1024]{1,2,0:T(8,128)(2,1)S(1)}, bf16[2,128,1024]{1,2,0:T(8,128)(2,1)}, u32[]{:S(2)}, u32[]{:S(2)}) collective-permute-start(bf16[2,128,1024]{1,2,0:T(8,128)(2,1)S(1)} %pad_maximum_fusion.1), channel_id=1, source_target_pairs={{0,3},{1,4},{2,5},{3,6},{4,7},{5,8},{6,9},{7,10},{8,11},{9,12},{10... | collective-permute-start | bytes 1572872 | tf_op jit(solution)/shard_map/ppermute | solution.py:14
  20.4 14.3 %collective-permute-start.2 = (bf16[2,128,1024]{1,2,0:T(8,128)(2,1)S(1)}, bf16[2,128,1024]{1,2,0:T(8,128)(2,1)}, u32[]{:S(2)}, u32[]{:S(2)}) collective-permute-start(bf16[2,128,1024]{1,2,0:T(8,128)(2,1)S(1)} %pad_maximum_fusion.1), channel_id=1, source_target_pairs={{0,2},{1,3},{2,4},{3,5},{4,6},{5,7},{6,8},{7,9},{8,10},{9,11},{10,... | collective-permute-start | bytes 1572872 | tf_op jit(solution)/shard_map/ppermute | solution.py:14
  22.7 22.4 %collective-permute-start.3 = (bf16[2,128,1024]{1,2,0:T(8,128)(2,1)S(1)}, bf16[2,128,1024]{1,2,0:T(8,128)(2,1)}, u32[]{:S(2)}, u32[]{:S(2)}) collective-permute-start(bf16[2,128,1024]{1,2,0:T(8,128)(2,1)S(1)} %pad_maximum_fusion.1), channel_id=1, source_target_pairs={{0,1},{1,2},{2,3},{3,4},{4,5},{5,6},{6,7},{7,8},{8,9},{9,10},{10,1... | collective-permute-start | bytes 1572872 | tf_op jit(solution)/shard_map/ppermute | solution.py:14
  76.0 5.8 copy-start.3
  86.4 5.2 copy-start.4
  97.7 158.1 %all-gather.14.cloned.1.call-start = ((), (), s32[]{:S(2)}) async-start(), calls=%async_computation.4 | async-start | bytes 2228224 | tf_op jit(solution)/shard_map/all_gather | solution.py:86
  98.5 193.1 %all-gather.10.cloned.1.call-start = ((), (), s32[]{:S(2)}) async-start(), calls=%async_computation.2 | async-start | bytes 2228224 | tf_op jit(solution)/shard_map/all_gather | solution.py:87
  99.2 245.9 %all-gather.18.cloned.1.call-start = ((), (), s32[]{:S(2)}) async-start(), calls=%async_computation.6 | async-start | bytes 8912896 | tf_op jit(solution)/shard_map/all_gather | solution.py:85
  99.2 126.9 %copy-start.6 = (f32[8192]{0:T(1024)S(1)}, f32[8192]{0:T(1024)}, u32[]{:S(2)}) copy-start(f32[8192]{0:T(1024)} %param.18) | copy-start | bytes 98308
  99.8 280.4 %all-gather.16.cloned.1.call-start = ((), (), s32[]{:S(2)}) async-start(), calls=%async_computation.5 | async-start | bytes 1114112 | tf_op jit(solution)/shard_map/all_gather | solution.py:100
  221.9 5.8 copy-start
  260.5 155.3 %all-gather.12.cloned.1.call-start = ((), (), s32[]{:S(2)}) async-start(), calls=%async_computation.3 | async-start | bytes 1114112 | tf_op jit(solution)/shard_map/all_gather | solution.py:101
  296.6 173.1 %all-gather.20.cloned.1.call-start = ((), (), s32[]{:S(2)}) async-start(), calls=%async_computation.7 | async-start | bytes 8912896 | tf_op jit(solution)/shard_map/all_gather | solution.py:128
  297.3 265.6 %reduce-scatter.2.cloned.1.call-start = ((), (), s32[]{:S(2)}) async-start(), calls=%async_computation.8 | async-start | bytes 4718592 | tf_op jit(solution)/shard_map/reduce_scatter | solution.py:129
  384.2 5.7 copy-start.1
  477.4 85.6 %copy-start.2 = (f32[32,8192]{1,0:T(8,128)S(1)}, f32[32,8192]{1,0:T(8,128)}, u32[]{:S(2)}) copy-start(f32[32,8192]{1,0:T(8,128)} %multiply_reduce_fusion.1) | copy-start | bytes 3145732
  477.4 91.6 %copy-start.5 = (f32[4,8192]{1,0:T(4,128)S(1)}, f32[4,8192]{1,0:T(4,128)}, u32[]{:S(2)}) copy-start(f32[4,8192]{1,0:T(4,128)} %param.23) | copy-start | bytes 393220
  564.1 4.7 collective-permute-start.4
Sparse Core Ops, SparseCore 0:
  97.8 124.0 all-gather.7
  223.6 32.0 all-gather.13
  257.5 33.9 all-gather.9
  293.1 51.9 all-gather.17
  346.6 33.5 all-gather.15
  381.7 34.0 all-gather.11
  417.5 52.1 all-gather.19
  477.5 85.3 reduce-scatter.1
where the time goes:
time: 596 us; the launch traced here: 590 us
  waiting for transfers between devices  419 us (70%)
  matrix products  66.7 us (11%)
  local copies, waits for them, and re-layouts  35.8 us (6%)
  other arithmetic  34.3 us (6%)
  starting transfers between devices  20.5 us (3%)
  between operations  13.7 us (2%)
    all_gather x1, waiting for transfers between devices, per_device(): block_f = lax.all_gather(pooled, 'tp', axis=0, tiled=True)  122 us
    reduce_scatter x1, waiting for transfers between devices, per_device(): lax.psum_scatter(jnp.dot(head_out, out_full, preferred_element_type=jnp.f...  85.5 us
    all_gather x1, waiting for transfers between devices, per_device(): lax.all_gather(w_query, 'ctx', axis=0, tiled=True)  47 us
    all_gather x1, waiting for transfers between devices, per_device(): out_full = lax.all_gather(w_out, 'ctx', axis=1, tiled=True)  43.5 us
    all_gather x1, waiting for transfers between devices, per_device(): lax.all_gather(w_value, 'ctx', axis=0, tiled=True)  30.9 us
    all_gather x1, waiting for transfers between devices, per_device(): key_piece = lax.all_gather(key_rows, 'ctx', axis=0, tiled=True)  28.1 us
    all_gather x1, waiting for transfers between devices, per_device(): lax.all_gather(w_key, 'ctx', axis=0, tiled=True)  25 us
    all_gather x1, waiting for transfers between devices, per_device(): value_piece = lax.all_gather(value_rows, 'ctx', axis=0, tiled=True)  21.7 us
  transfers between devices with their start and end apart: 13, of which 11 were waited for; matrix products, arithmetic and copies ran while one was open for 9% of the time, Pallas kernels for 0%

commit v1 on v0

v1 whole, which is shorter than its diff:
```python
import functools

import jax
import jax.numpy as jnp
from jax import lax
from jax.experimental import pallas as pl
from jax.experimental.pallas import tpu as pltpu
from jax.sharding import PartitionSpec as P

HEAD = 128
WIN = 512
POOL = 4
LOG2E = 1.4426950408889634
MESH = pl.DeviceIdType.MESH
F32 = jnp.float32
BF16 = jnp.bfloat16
VMEM_SPEC = pl.BlockSpec(memory_space=pltpu.VMEM)
ANY_SPEC = pl.BlockSpec(memory_space=pl.ANY)


def lanes(start, size):
    return pl.ds(pl.multiple_of(start, 128), size)


def fine_kernel(
    n_tp, n_dev, chunks, q_ref, k_ref, v_ref, x_ref, win_ref, pw_ref, gain_ref,
    stream_ref, pooled_ref, a_full, rs_full,
    kbuf, vbuf, dist, a_send, rs_send, ssq,
    hs_sem, hr_sem, as_sem, ar_sem, rss_sem, rsr_sem, loc_sem,
):
    rows = q_ref.shape[0]
    width = q_ref.shape[1]
    kv_width = k_ref.shape[1]
    reach = WIN // rows
    span = (reach + 1) * rows
    group = width // kv_width
    pool_rows = rows // POOL
    kv_chunk = kv_width // chunks
    q_chunk = width // chunks
    ctx = lax.axis_index("ctx")
    tp = lax.axis_index("tp")
    me = ctx * n_tp + tp

    def along(step):
        other = lax.rem(me + step + n_dev, n_dev)
        return (other // n_tp, lax.rem(other, n_tp))

    def peer(step):
        return (ctx, lax.rem(tp + step, n_tp))

    barrier = pltpu.get_barrier_semaphore()
    for d in range(1, reach + 1):
        pl.semaphore_signal(barrier, inc=1, device_id=along(-d), device_id_type=MESH)
    for d in range(1, n_tp):
        pl.semaphore_signal(barrier, inc=1, device_id=peer(d), device_id_type=MESH)
    pl.semaphore_wait(barrier, reach + n_tp - 1)

    def halo(hc, d, which):
        src, dst = ((k_ref, kbuf), (v_ref, vbuf))[which]
        cols = lanes(hc * kv_chunk, kv_chunk)
        return pltpu.make_async_remote_copy(
            src_ref=src.at[:, cols],
            dst_ref=dst.at[pl.ds((reach - d) * rows, rows), cols],
            send_sem=hs_sem.at[which, hc, d - 1],
            recv_sem=hr_sem.at[which, hc, d - 1],
            device_id=along(d),
            device_id_type=MESH,
        )

    for hc in range(chunks):
        for which in range(2):
            for d in range(1, reach + 1):
                halo(hc, d, which).start()

    kbuf[reach * rows :, :] = k_ref[...]
    vbuf[reach * rows :, :] = v_ref[...]
    q_at = lax.broadcasted_iota(jnp.int32, (rows, span), 0)
    l_at = lax.broadcasted_iota(jnp.int32, (rows, span), 1)
    gap = reach * rows + q_at - l_at
    outside = (gap < 0) | (l_at < (reach - me) * rows)
    dist[...] = jnp.where(outside, 2 * span, gap)
    ssq[...] = jnp.zeros_like(ssq)

    def a_copy(hc, step):
        cols = lanes(hc * q_chunk, q_chunk)
        return pltpu.make_async_remote_copy(
            src_ref=a_send.at[:, cols],
            dst_ref=a_full.at[tp, :, cols],
            send_sem=as_sem.at[hc, step],
            recv_sem=ar_sem.at[hc, tp],
            device_id=peer(step),
            device_id_type=MESH,
        )

    def a_arrival(hc, step):
        src_tp = lax.rem(tp + step, n_tp)
        cols = lanes(hc * q_chunk, q_chunk)
        return pltpu.make_async_remote_copy(
            src_ref=a_send.at[:, cols],
            dst_ref=a_full.at[src_tp, :, cols],
            send_sem=as_sem.at[hc, step],
            recv_sem=ar_sem.at[hc, src_tp],
            device_id=peer(step),
            device_id_type=MESH,
        )

    half = group // 2

    def chunk(hc, carry):
        for which in range(2):
            for d in range(1, reach + 1):
                halo(hc, d, which).wait_recv()
        for u in range(kv_chunk // HEAD):
            kv_cols = lanes(hc * kv_chunk + u * HEAD, HEAD)
            keys = kbuf[:, kv_cols]
            values = vbuf[:, kv_cols]
            for part in range(2):
                first = (hc * (kv_chunk // HEAD) + u) * group + part * half
                qs = jnp.concatenate(
                    [q_ref[:, lanes((first + i) * HEAD, HEAD)] for i in range(half)], axis=0
                )
                scores = lax.dot_general(
                    qs, keys, (((1,), (1,)), ((), ())), preferred_element_type=F32
                )
                weights, totals = [], []
                for i in range(half):
                    s = scores[i * rows : (i + 1) * rows] * (LOG2E * HEAD**-0.5)
                    s = jnp.where(dist[...] < win_ref[first + i], s, -1e30)
                    p = jnp.exp2(s - s.max(-1, keepdims=True))
                    totals.append(p.sum(-1, keepdims=True))
                    weights.append(p.astype(BF16))
                mixed = jnp.dot(
                    jnp.concatenate(weights, axis=0), values, preferred_element_type=F32
                )
                for i in range(half):
                    cols = lanes((first + i) * HEAD, HEAD)
                    stream_ref[first + i] = (
                        x_ref[:, cols].astype(F32) + mixed[i * rows : (i + 1) * rows] / totals[i]
                    )
        for i in range(q_chunk // HEAD):
            cols = lanes(hc * q_chunk + i * HEAD, HEAD)
            head = hc * (q_chunk // HEAD) + i
            pooled = sum(
                pw_ref[j : j + 1, cols] * stream_ref[head, pl.ds(j, pool_rows, stride=POOL), :]
                for j in range(POOL)
            )
            pooled_ref[:, cols] = pooled
            ssq[...] += pooled * pooled
            a_send[:, cols] = (pooled * gain_ref[:, cols]).astype(BF16)
        for step in range(1, n_tp):
            a_copy(hc, step).start()
        return carry

    lax.fori_loop(0, chunks, chunk, 0)

    mean = ssq[...].sum(-1, keepdims=True) * (1.0 / width)
    rs_send[...] = jnp.broadcast_to(lax.rsqrt(mean + 1e-05), rs_send.shape)

    def rs_copy(step):
        return pltpu.make_async_remote_copy(
            src_ref=rs_send,
            dst_ref=rs_full.at[tp],
            send_sem=rss_sem.at[step],
            recv_sem=rsr_sem.at[tp],
            device_id=peer(step),
            device_id_type=MESH,
        )

    def rs_arrival(step):
        src_tp = lax.rem(tp + step, n_tp)
        return pltpu.make_async_remote_copy(
            src_ref=rs_send,
            dst_ref=rs_full.at[src_tp],
            send_sem=rss_sem.at[step],
            recv_sem=rsr_sem.at[src_tp],
            device_id=peer(step),
            device_id_type=MESH,
        )

    for step in range(1, n_tp):
        rs_copy(step).start()
    own_a = pltpu.make_async_copy(a_send, a_full.at[tp], loc_sem.at[0])
    own_rs = pltpu.make_async_copy(rs_send, rs_full.at[tp], loc_sem.at[1])
    own_a.start()
    own_rs.start()
    own_a.wait()
    own_rs.wait()
    for hc in range(chunks):
        for which in range(2):
            for d in range(1, reach + 1):
                halo(hc, d, which).wait_send()
        for step in range(1, n_tp):
            a_copy(hc, step).wait_send()
            a_arrival(hc, step).wait_recv()
    for step in range(1, n_tp):
        rs_copy(step).wait_send()
        rs_arrival(step).wait_recv()


def fine_stage(mesh, fine_q, fine_k, fine_v, fine_x, windows, pool_w, gain):
    rows, width = fine_q.shape
    kv_width = fine_k.shape[1]
    n_tp = mesh.shape["tp"]
    n_dev = n_tp * mesh.shape["ctx"]
    chunks = 4
    reach = WIN // rows
    span = (reach + 1) * rows
    pool_rows = rows // POOL
    return pl.pallas_call(
        functools.partial(fine_kernel, n_tp, n_dev, chunks),
        out_shape=[
            jax.ShapeDtypeStruct((width // HEAD, rows, HEAD), F32),
            jax.ShapeDtypeStruct((pool_rows, width), F32),
            jax.ShapeDtypeStruct((n_tp, pool_rows, width), BF16),
            jax.ShapeDtypeStruct((n_tp, pool_rows, HEAD), F32),
        ],
        in_specs=[VMEM_SPEC] * 4 + [pl.BlockSpec(memory_space=pltpu.SMEM)] + [VMEM_SPEC] * 2,
        out_specs=[VMEM_SPEC, VMEM_SPEC, ANY_SPEC, ANY_SPEC],
        scratch_shapes=[
            pltpu.VMEM((span, kv_width), BF16),
            pltpu.VMEM((span, kv_width), BF16),
            pltpu.VMEM((rows, span), jnp.int32),
            pltpu.VMEM((pool_rows, width), BF16),
            pltpu.VMEM((pool_rows, HEAD), F32),
            pltpu.VMEM((pool_rows, HEAD), F32),
            pltpu.SemaphoreType.DMA((2, chunks, reach)),
            pltpu.SemaphoreType.DMA((2, chunks, reach)),
            pltpu.SemaphoreType.DMA((chunks, n_tp)),
            pltpu.SemaphoreType.DMA((chunks, n_tp)),
            pltpu.SemaphoreType.DMA((n_tp,)),
            pltpu.SemaphoreType.DMA((n_tp,)),
            pltpu.SemaphoreType.DMA((2,)),
        ],
        compiler_params=pltpu.CompilerParams(
            collective_id=0, has_side_effects=True, vmem_limit_bytes=40 * 2**20
        ),
        cost_estimate=pl.CostEstimate(
            flops=60_000_000_000, bytes_accessed=20 * 2**20, transcendentals=0
        ),
        name="fine_stage",
    )(fine_q, fine_k, fine_v, fine_x, windows, pool_w, gain)


def coarse_kernel(
    n_chip, a_hbm, rs_ref, w_hbm, out_ref,
    a_v, w_v, acc, kv_all, q_all, top, total, mixed,
    a_sem, w_sem, ds_sem, dr_sem, fs_sem, fr_sem,
):
    rows = a_v.shape[0]
    steps = a_sem.shape[0]
    depth = a_v.shape[1] // steps
    q_width = out_ref.shape[1]
    heads = q_width // HEAD
    ctx = lax.axis_index("ctx")
    tp = lax.axis_index("tp")
    chip = ctx // 2
    core = lax.rem(ctx, 2)
    sibling = chip * 2 + 1 - core

    barrier = pltpu.get_barrier_semaphore()
    for d in range(1, n_chip):
        other = lax.rem(chip + d, n_chip) * 2 + core
        pl.semaphore_signal(barrier, inc=1, device_id=(other, tp), device_id_type=MESH)
    pl.semaphore_signal(barrier, inc=1, device_id=(sibling, tp), device_id_type=MESH)

    def loads(k):
        return (
            pltpu.make_async_copy(
                a_hbm.at[:, lanes(k * depth, depth)], a_v.at[:, lanes(k * depth, depth)], a_sem.at[k]
            ),
            pltpu.make_async_copy(
                w_hbm.at[lanes(k * depth, depth)], w_v.at[lanes(k * depth, depth)], w_sem.at[k]
            ),
        )

    for k in range(steps):
        for load in loads(k):
            load.start()
    acc[...] = jnp.zeros_like(acc)

    def project(k, carry):
        for load in loads(k):
            load.wait()
        acc[...] += jnp.dot(
            a_v[:, lanes(k * depth, depth)],
            w_v[lanes(k * depth, depth), :],
            preferred_element_type=F32,
        )
        return carry

    lax.fori_loop(0, steps, project, 0)
    row_scale = rs_ref[:, 0:1]
    kv_all[ctx] = (acc[:, q_width:] * row_scale).astype(BF16)

    pl.semaphore_wait(barrier, n_chip)

    def direct(to_chip):
        return pltpu.make_async_remote_copy(
            src_ref=kv_all.at[ctx],
            dst_ref=kv_all.at[ctx],
            send_sem=ds_sem.at[to_chip],
            recv_sem=dr_sem.at[chip],
            device_id=(to_chip * 2 + core, tp),
            device_id_type=MESH,
        )

    def direct_arrival(from_chip):
        return pltpu.make_async_remote_copy(
            src_ref=kv_all.at[ctx],
            dst_ref=kv_all.at[from_chip * 2 + core],
            send_sem=ds_sem.at[from_chip],
            recv_sem=dr_sem.at[from_chip],
            device_id=(from_chip * 2 + core, tp),
            device_id_type=MESH,
        )

    def across(from_chip):
        return pltpu.make_async_remote_copy(
            src_ref=kv_all.at[from_chip * 2 + core],
            dst_ref=kv_all.at[from_chip * 2 + core],
            send_sem=fs_sem.at[from_chip],
            recv_sem=fr_sem.at[from_chip],
            device_id=(sibling, tp),
            device_id_type=MESH,
        )

    def across_arrival(from_chip):
        return pltpu.make_async_remote_copy(
            src_ref=kv_all.at[from_chip * 2 + core],
            dst_ref=kv_all.at[from_chip * 2 + 1 - core],
            send_sem=fs_sem.at[from_chip],
            recv_sem=fr_sem.at[from_chip],
            device_id=(sibling, tp),
            device_id_type=MESH,
        )

    def send(b, carry):
        direct(b).start()
        return carry

    across(chip).start()
    lax.fori_loop(chip + 1, n_chip, send, 0)

    for h in range(heads):
        q_all[h] = (acc[:, h * HEAD : (h + 1) * HEAD] * row_scale).astype(BF16)

    def attend(b, first):
        keys = jnp.concatenate([kv_all[2 * b, :, :HEAD], kv_all[2 * b + 1, :, :HEAD]], axis=0)
        values = jnp.concatenate([kv_all[2 * b, :, HEAD:], kv_all[2 * b + 1, :, HEAD:]], axis=0)
        for h in range(heads):
            s = lax.dot_general(
                q_all[h], keys, (((1,), (1,)), ((), ())), preferred_element_type=F32
            ) * (LOG2E * HEAD**-0.5)
            if first:
                q_at = core * rows + lax.broadcasted_iota(jnp.int32, s.shape, 0)
                k_at = lax.broadcasted_iota(jnp.int32, s.shape, 1)
                s = jnp.where(k_at <= q_at, s, -1e30)
                new_top = s.max(-1, keepdims=True)
                p = jnp.exp2(s - new_top)
                total[h] = p.sum(-1, keepdims=True)
                mixed[h] = jnp.dot(p.astype(BF16), values, preferred_element_type=F32)
            else:
                old = top[h]
                new_top = jnp.maximum(old, s.max(-1, keepdims=True))
                keep = jnp.exp2(old - new_top)
                p = jnp.exp2(s - new_top)
                total[h] = total[h] * keep + p.sum(-1, keepdims=True)
                mixed[h] = mixed[h] * keep + jnp.dot(
                    p.astype(BF16), values, preferred_element_type=F32
                )
            top[h] = new_top

    across_arrival(chip).wait_recv()
    attend(chip, True)

    def forward(b, carry):
        direct_arrival(b).wait_recv()
        across(b).start()
        return carry

    lax.fori_loop(0, chip, forward, 0)

    def earlier(b, carry):
        across_arrival(b).wait_recv()
        attend(b, False)
        return carry

    lax.fori_loop(0, chip, earlier, 0)
    for h in range(heads):
        out_ref[:, h * HEAD : (h + 1) * HEAD] = (mixed[h] / total[h]).astype(BF16)

    def drain_direct(b, carry):
        direct(b).wait_send()
        return carry

    def drain_across(b, carry):
        across(b).wait_send()
        return carry

    lax.fori_loop(chip + 1, n_chip, drain_direct, 0)
    lax.fori_loop(0, chip + 1, drain_across, 0)


def coarse_stage(mesh, a_full, rs_full, w_full, q_width):
    rows, width = a_full.shape
    n_ctx = mesh.shape["ctx"]
    steps = 16
    kv2 = w_full.shape[1] - q_width
    heads = q_width // HEAD
    return pl.pallas_call(
        functools.partial(coarse_kernel, n_ctx // 2),
        out_shape=jax.ShapeDtypeStruct((rows, q_width), BF16),
        in_specs=[ANY_SPEC, VMEM_SPEC, ANY_SPEC],
        out_specs=VMEM_SPEC,
        scratch_shapes=[
            pltpu.VMEM((rows, width), BF16),
            pltpu.VMEM(w_full.shape, BF16),
            pltpu.VMEM((rows, w_full.shape[1]), F32),
            pltpu.VMEM((n_ctx, rows, kv2), BF16),
            pltpu.VMEM((heads, rows, HEAD), BF16),
            pltpu.VMEM((heads, rows, 1), F32),
            pltpu.VMEM((heads, rows, 1), F32),
            pltpu.VMEM((heads, rows, HEAD), F32),
            pltpu.SemaphoreType.DMA((steps,)),
            pltpu.SemaphoreType.DMA((steps,)),
            pltpu.SemaphoreType.DMA((n_ctx // 2,)),
            pltpu.SemaphoreType.DMA((n_ctx // 2,)),
            pltpu.SemaphoreType.DMA((n_ctx // 2,)),
            pltpu.SemaphoreType.DMA((n_ctx // 2,)),
        ],
        compiler_params=pltpu.CompilerParams(
            collective_id=1, has_side_effects=True, vmem_limit_bytes=40 * 2**20
        ),
        cost_estimate=pl.CostEstimate(
            flops=40_000_000_000, bytes_accessed=20 * 2**20, transcendentals=0
        ),
        name="coarse_stage",
    )(a_full, rs_full, w_full)


def out_kernel(
    n_tp, n_dev, heads_ref, pooled_ref, w_hbm, shifted_ref,
    w_v, sent, got, coarse, last_send, last_got,
    w_sem, s_sem, r_sem, l_sem,
):
    rows = heads_ref.shape[0]
    own = pooled_ref.shape[0]
    blocks, depth, cols = w_v.shape
    groups = s_sem.shape[0]
    per = blocks // groups
    ctx = lax.axis_index("ctx")
    tp = lax.axis_index("tp")
    me = ctx * n_tp + tp

    def along(step):
        other = lax.rem(me + step + n_dev, n_dev)
        return (other // n_tp, lax.rem(other, n_tp))

    def peer(step):
        return (ctx, lax.rem(tp + step, n_tp))

    barrier = pltpu.get_barrier_semaphore()
    for d in range(1, n_tp):
        pl.semaphore_signal(barrier, inc=1, device_id=peer(d), device_id_type=MESH)
    pl.semaphore_signal(barrier, inc=1, device_id=along(-1), device_id_type=MESH)

    def load(b):
        return pltpu.make_async_copy(w_hbm.at[b], w_v.at[b], w_sem.at[b])

    for b in range(blocks):
        load(b).start()

    pl.semaphore_wait(barrier, n_tp)

    def partial_copy(g, step):
        to = lax.rem(tp + step, n_tp)
        where = lanes(g * per * cols, per * cols)
        return pltpu.make_async_remote_copy(
            src_ref=sent.at[to, :, where],
            dst_ref=got.at[tp, :, where],
            send_sem=s_sem.at[g, step],
            recv_sem=r_sem.at[g, tp],
            device_id=peer(step),
            device_id_type=MESH,
        )

    def partial_arrival(g, step):
        source = lax.rem(tp + step, n_tp)
        where = lanes(g * per * cols, per * cols)
        return pltpu.make_async_remote_copy(
            src_ref=sent.at[source, :, where],
            dst_ref=got.at[source, :, where],
            send_sem=s_sem.at[g, step],
            recv_sem=r_sem.at[g, source],
            device_id=peer(step),
            device_id_type=MESH,
        )

    def multiply(g, carry):
        for i in range(per):
            b = g * per + i
            load(b).wait()
            product = jnp.dot(heads_ref[...], w_v[b], preferred_element_type=F32).astype(BF16)
            for p in range(n_tp):
                sent[p, :, lanes(b * cols, cols)] = product[p * own : (p + 1) * own]
        for step in range(1, n_tp):
            partial_copy(g, step).start()
        return carry

    lax.fori_loop(0, groups, multiply, 0)

    def gather(g, carry):
        where = lanes(g * per * cols, per * cols)
        for step in range(1, n_tp):
            partial_arrival(g, step).wait_recv()
        value = pooled_ref[:, where] + sent[tp, :, where].astype(F32)
        for step in range(1, n_tp):
            value += got[lax.rem(tp + step, n_tp), :, where].astype(F32)
        coarse[:, where] = value
        return carry

    lax.fori_loop(0, groups, gather, 0)

    piece = last_send.shape[1]
    for i in range(last_send.shape[0]):
        last_send[i : i + 1, :] = coarse[own - 1 : own, i * piece : (i + 1) * piece]
    last = pltpu.make_async_remote_copy(
        src_ref=last_send,
        dst_ref=last_got,
        send_sem=l_sem.at[0],
        recv_sem=l_sem.at[1],
        device_id=along(1),
        device_id_type=MESH,
    )
    last.start()
    shifted_ref[1:own, :] = coarse[0 : own - 1, :]
    last.wait()
    first_row = jnp.where(me == 0, 0.0, last_got[...])
    for i in range(last_send.shape[0]):
        shifted_ref[0:1, i * piece : (i + 1) * piece] = first_row[i : i + 1, :]

    def drain(g, carry):
        for step in range(1, n_tp):
            partial_copy(g, step).wait_send()
        return carry

    lax.fori_loop(0, groups, drain, 0)


def out_stage(mesh, heads, pooled, w_full):
    own, width = pooled.shape
    n_tp = mesh.shape["tp"]
    n_dev = n_tp * mesh.shape["ctx"]
    groups = 8
    blocks = w_full.shape[0]
    return pl.pallas_call(
        functools.partial(out_kernel, n_tp, n_dev),
        out_shape=jax.ShapeDtypeStruct((own, width), F32),
        in_specs=[VMEM_SPEC, VMEM_SPEC, ANY_SPEC],
        out_specs=VMEM_SPEC,
        scratch_shapes=[
            pltpu.VMEM(w_full.shape, BF16),
            pltpu.VMEM((n_tp, own, width), BF16),
            pltpu.VMEM((n_tp, own, width), BF16),
            pltpu.VMEM((own, width), F32),
            pltpu.VMEM((8, width // 8), F32),
            pltpu.VMEM((8, width // 8), F32),
            pltpu.SemaphoreType.DMA((blocks,)),
            pltpu.SemaphoreType.DMA((groups, n_tp)),
            pltpu.SemaphoreType.DMA((groups, n_tp)),
            pltpu.SemaphoreType.DMA((2,)),
        ],
        compiler_params=pltpu.CompilerParams(
            collective_id=2, has_side_effects=True, vmem_limit_bytes=40 * 2**20
        ),
        cost_estimate=pl.CostEstimate(
            flops=40_000_000_000, bytes_accessed=20 * 2**20, transcendentals=0
        ),
        name="out_stage",
    )(heads, pooled, w_full)


def combine_kernel(stream_ref, shifted_ref, up_ref, out_ref, spread):
    pool_rows = shifted_ref.shape[0]
    for i in range(stream_ref.shape[0]):
        cols = slice(i * HEAD, (i + 1) * HEAD)
        shifted = shifted_ref[:, cols]
        for j in range(POOL):
            spread[i, pl.ds(j, pool_rows, stride=POOL), :] = up_ref[j : j + 1, cols] * shifted
        out_ref[:, cols] = stream_ref[i] + spread[i]


def combine_stage(stream, shifted, up_w):
    n_heads, rows, _ = stream.shape
    width = n_heads * HEAD
    block = 1024
    per = block // HEAD
    return pl.pallas_call(
        combine_kernel,
        out_shape=jax.ShapeDtypeStruct((rows, width), F32),
        grid=(width // block,),
        in_specs=[
            pl.BlockSpec((per, rows, HEAD), lambda i: (i, 0, 0)),
            pl.BlockSpec((shifted.shape[0], block), lambda i: (0, i)),
            pl.BlockSpec((up_w.shape[0], block), lambda i: (0, i)),
        ],
        out_specs=pl.BlockSpec((rows, block), lambda i: (0, i)),
        scratch_shapes=[pltpu.VMEM((per, rows, HEAD), F32)],
        name="combine_stage",
    )(stream, shifted, up_w)


def per_device(
    mesh, fine_x, fine_q, fine_k, fine_v, windows, pool_w, norm_gain, w_query, w_key, w_value, w_out, up_w
):
    w_local = jnp.concatenate([w_query, w_key, w_value], axis=1)
    w_full = lax.all_gather(w_local, "ctx", axis=0, tiled=True)
    out_full = lax.all_gather(w_out, "ctx", axis=0, tiled=False)
    stream, pooled, a_full, rs_full = fine_stage(
        mesh, fine_q, fine_k, fine_v, fine_x, windows, pool_w, norm_gain[None]
    )
    a_rows = a_full.reshape(-1, a_full.shape[-1])
    rs_rows = rs_full.reshape(-1, rs_full.shape[-1])
    heads = coarse_stage(mesh, a_rows, rs_rows, w_full, w_query.shape[1])
    shifted = out_stage(mesh, heads, pooled, out_full)
    return combine_stage(stream, shifted, up_w)


def solution(mesh):
    placed = (
        P(("ctx", "tp"), None),
        P(("ctx", "tp"), None),
        P(("ctx", "tp"), None),
        P(("ctx", "tp"), None),
        P(),
        P(),
        P(),
        P("ctx", "tp"),
        P("ctx", "tp"),
        P("ctx", "tp"),
        P("tp", "ctx"),
        P(),
    )
    return jax.shard_map(
        functools.partial(per_device, mesh),
        mesh=mesh,
        in_specs=placed,
        out_specs=P(("ctx", "tp"), None),
        check_vma=False,
    )
```

time: 596 us -> 315 us (0.53)
  waiting for transfers between devices: 419 us -> 0.73 us
  Pallas kernels: 0 us -> 284 us
  matrix products: 66.7 us -> 0 us
  other arithmetic: 34.3 us -> 2.25 us
  local copies, waits for them, and re-layouts: 35.8 us -> 13.3 us
  starting transfers between devices: 20.5 us -> 0.08 us
    all_gather x7 -> x2, waiting for transfers between devices: 318 us -> 0.02 us  [the longest x1 0.02 us: per_device(): out_full = lax.all_gather(w_out, 'ctx', axis=0, tiled=False)]
    pallas_call x0 -> x4, Pallas kernels: none -> 284 us  [the longest x1 173 us: fine_stage(): pl.pallas_call(functools.partial(fine_kernel, n_tp, n_dev, chunks), out_s...]
    reduce_scatter x1 -> x0, waiting for transfers between devices: 85.5 us -> none  [per_device(): lax.psum_scatter(jnp.dot(head_out, out_full, preferred_element_type=jnp.f...]
    dot_general x7 -> x0, matrix products: 47 us -> none  [the longest x1 10.4 us: per_device(): jnp.einsum('kgql,lkd->qkgd', weights.astype(jnp.bfloat16), value_piece.re...]
    ppermute x5 -> x0, starting transfers between devices: 20.2 us -> none  [passed_along(): return lax.ppermute(block, axis, route)]
    sub x1 -> x0, matrix products: 19.7 us -> none  [attend_window(): weights = jnp.where(allowed, jnp.exp(scores - row_top), 0.0)]
    reduce_sum x3 -> x0, other arithmetic: 14.4 us -> none  [the longest x1 6.03 us: per_device(): (stream.reshape(pool_rows, POOL, model_width) * pool_w[None]).sum(1)]
    ppermute x5 -> x0, waiting for transfers between devices: 12.9 us -> none  [passed_along(): return lax.ppermute(block, axis, route)]
  transfers between devices with their start and end apart: 13 -> 2, of which waited for: 11 -> 0; matrix products, arithmetic and copies ran while one was open for 9% -> 0% of each run, Pallas kernels for 0% -> 61%
where the time goes in v1:
time: 315 us; the launch traced here: 314 us
  Pallas kernels  284 us (90%)
  between operations  13.5 us (4%)
  local copies, waits for them, and re-layouts  13.3 us (4%)
    pallas_call x1, Pallas kernels, fine_stage(): pl.pallas_call(functools.partial(fine_kernel, n_tp, n_dev, chunks), out_s...  173 us
    pallas_call x1, Pallas kernels, out_stage(): pl.pallas_call(functools.partial(out_kernel, n_tp, n_dev), out_shape=jax....  86 us
    pallas_call x1, Pallas kernels, coarse_stage(): pl.pallas_call(functools.partial(coarse_kernel, n_ctx // 2), out_shape=ja...  18.7 us
    unnamed x28, local copies, waits for them, and re-layouts  13.3 us
    pallas_call x1, Pallas kernels, combine_stage(): pl.pallas_call(combine_kernel, out_shape=jax.ShapeDtypeStruct((rows, widt...  7.14 us
  transfers between devices with their start and end apart: 2, of which 0 were waited for; matrix products, arithmetic and copies ran while one was open for 0% of the time, Pallas kernels for 61%

profile of v1, /device:TPU:0, one launch (start us, length us, event | category | flops | bytes accessed | tf_op | source)
XLA Modules:
  0.0 314.3 jit_solution(17974411137906476916)
XLA Ops:
  6.5 0.0 copy-start.8
  6.5 0.0 copy-start.3
  6.5 0.0 copy-start.5
  6.5 0.0 copy-start.6
  6.5 0.0 copy-start.9
  6.5 0.0 copy-start.7
  6.6 0.0 all-gather.4.cloned.1.call-start
  6.6 2.2 pad_maximum_fusion
  8.9 0.0 all-gather.4.cloned.1.call-update
  8.9 0.0 all-gather.6.cloned.1.call-start
  8.9 0.7 all-gather.6.cloned.1.call-update
  9.6 0.0 copy-done.8
  9.6 0.0 copy-done.3
  9.7 0.0 copy-done.5
  9.7 0.0 copy-done.6
  9.7 0.0 copy-done.9
  9.7 0.0 copy-done.7
  9.7 0.0 copy-start.4
  9.7 1.6 copy-done.4
  11.3 172.6 %fine_stage.1 = (f32[64,128,128]{2,1,0:T(8,128)S(1)}, f32[32,8192]{1,0:T(8,128)S(1)}, bf16[8,32,8192]{2,1,0:T(8,128)(2,1)S(1)}, f32[8,32,128]{2,1,0:T(8,128)S(1)}) custom-call(bf16[128,8192]{1,0:T(8,128)(2,1)S(1)} %copy-done.3, bf16[128,1024]{1,0:T(8,128)(2,1)S(1)} %copy-done.5, bf16[128,1024]{1,0:T(8,128)(2,1)S(1)} %copy-done.6, ...), custom_call_target="tpu_custom_call" | custom-call | flops 60000002048 | bytes 20971520 | tf_op jit(solution)/shard_map/fine_stage/pallas_call | solution.py:209
  183.9 0.0 copy-start
  183.9 2.0 copy-done
  185.9 0.0 copy-start.10
  185.9 2.0 copy-done.10
  187.9 0.0 copy-start.12
  187.9 1.1 copy-done.12
  188.9 0.0 all-gather.4.cloned.1.call-done.w_hbm
  188.9 0.0 copy-start.11
  188.9 2.2 copy-done.11
  191.2 0.0 copy-start.13
  191.2 18.7 %coarse_stage.1.heads_ref = bf16[256,512]{1,0:T(8,128)(2,1)S(1)} custom-call(bf16[256,8192]{1,0:T(8,128)(2,1)S(1)} %bitcast.6, f32[256,128]{1,0:T(8,128)S(1)} %bitcast.7, bf16[8192,768]{1,0:T(8,128)(2,1)} %all-gather.4.cloned.1.call-done.w_hbm), custom_call_target="tpu_custom_call" | custom-call | flops 40000000000 | bytes 20971520 | tf_op jit(solution)/shard_map/coarse_stage/pallas_call | solution.py:410
  209.9 0.0 all-gather.6.cloned.1.call-done
  209.9 0.0 copy-done.13
  209.9 0.0 copy-start.2
  209.9 3.4 %copy-done.2 = bf16[8192,512]{1,0:T(8,128)(2,1)S(1)} copy-done((bf16[8192,512]{1,0:T(8,128)(2,1)S(1)}, bf16[8192,512]{1,0:T(8,128)(2,1)}, u32[]{:S(2)}) %copy-start.2) | copy-done | bytes 8388632
  213.3 86.0 %out_stage.1.shifted_ref = f32[32,8192]{1,0:T(8,128)S(1)} custom-call(bf16[256,512]{1,0:T(8,128)(2,1)S(1)} %coarse_stage.1.heads_ref, f32[32,8192]{1,0:T(8,128)S(1)} %copy-done.13, bf16[16,512,512]{2,1,0:T(8,128)(2,1)S(1)} %bitcast.4), custom_call_target="tpu_custom_call" | custom-call | flops 40000000000 | bytes 20971520 | tf_op jit(solution)/shard_map/out_stage/pallas_call | solution.py:556
  299.3 0.0 copy-start.1
  299.3 1.0 copy-done.1
  300.3 7.1 %combine_stage.1 = f32[128,8192]{1,0:T(8,128)} custom-call(f32[64,128,128]{2,1,0:T(8,128)} %copy-done, f32[32,8192]{1,0:T(8,128)} %copy-done.1, f32[4,8192]{1,0:T(4,128)} %up_ref.1), custom_call_target="tpu_custom_call" | custom-call | tf_op jit(solution)/shard_map/combine_stage/pallas_call | solution.py:598
Async XLA Ops:
  6.5 3.1 copy-start.8
  6.5 3.1 copy-start.3
  6.5 3.1 copy-start.5
  6.5 3.1 copy-start.6
  6.5 3.1 copy-start.9
  6.5 3.1 copy-start.7
  6.6 182.4 %all-gather.4.cloned.1.call-start = ((), (), s32[]{:S(2)}) async-start(), calls=%async_computation | async-start | bytes 13369344 | tf_op jit(solution)/shard_map/all_gather | solution.py:617
  8.9 201.0 %all-gather.6.cloned.1.call-start = ((), (), s32[]{:S(2)}) async-start(), calls=%async_computation.1 | async-start | bytes 8912896 | tf_op jit(solution)/shard_map/all_gather | solution.py:618
  9.7 1.6 copy-start.4
  183.9 2.0 copy-start
  185.9 2.0 copy-start.10
  187.9 1.1 copy-start.12
  188.9 2.2 copy-start.11
  191.2 18.7 %copy-start.13 = (f32[32,8192]{1,0:T(8,128)S(1)}, f32[32,8192]{1,0:T(8,128)}, u32[]{:S(2)}) copy-start(f32[32,8192]{1,0:T(8,128)} %copy-done.12) | copy-start | bytes 3145732
  209.9 3.4 %copy-start.2 = (bf16[8192,512]{1,0:T(8,128)(2,1)S(1)}, bf16[8192,512]{1,0:T(8,128)(2,1)}, u32[]{:S(2)}) copy-start(bf16[8192,512]{1,0:T(8,128)(2,1)} %all-gather.6.cloned.1.call-done) | copy-start | bytes 25165828
  299.3 1.0 copy-start.1
Sparse Core Ops, SparseCore 0:
  9.1 127.7 all-gather.3
  138.6 56.4 all-gather.5

commit v2 on v0

v2 whole, which is shorter than its diff:
```python
import functools

import jax
import jax.numpy as jnp
from jax import lax
from jax.experimental import pallas as pl
from jax.experimental.pallas import tpu as pltpu
from jax.sharding import PartitionSpec as P

HEAD = 128
WIN = 512
POOL = 4
RING = 4
LOG2E = 1.4426950408889634
MESH = pl.DeviceIdType.MESH
F32 = jnp.float32
BF16 = jnp.bfloat16
VMEM_SPEC = pl.BlockSpec(memory_space=pltpu.VMEM)
ANY_SPEC = pl.BlockSpec(memory_space=pl.ANY)
CHUNKS = 4
GROUPS = 8


def lanes(start, size):
    return pl.ds(pl.multiple_of(start, 128), size)


def sublanes(start, size):
    return pl.ds(pl.multiple_of(start, size), size)


def block_kernel(
    q_ref, k_ref, v_ref, x_ref, win_ref, pw_ref, gain_ref, up_ref, wq_hbm, wk_hbm, wv_hbm, wo_hbm,
    out_hbm,
    kbuf, vbuf, dist, stream, pooled_v, a_full, rs_all, ssq,
    w_all, wo_all, acc, kv_all, q_all, top, total, mixed, heads_v,
    keep, s_send, s_got, y_send, y_got, shifted, last_send, last_got,
    hs_sem, hr_sem, as_sem, ar_sem, af_sem, rss_sem, rsr_sem,
    ho_sem, wgs_sem, wgr_sem, kvs_sem, kvr_sem,
    ss_sem, sr_sem, ys_sem, yr_sem, l_sem, o_sem,
):
    rows, width = q_ref.shape
    kv_width = k_ref.shape[1]
    reach = WIN // rows
    span = (reach + 1) * rows
    group = width // kv_width
    own = rows // POOL
    kv_chunk = kv_width // CHUNKS
    q_chunk = width // CHUNKS
    n_ctx = w_all.shape[0]
    depth = w_all.shape[1]
    half = depth // 2
    q_width = heads_v.shape[1]
    heads = q_width // HEAD
    all_rows = heads_v.shape[0]
    n_tp = 2 * RING
    n_dev = n_ctx * n_tp

    ctx = lax.axis_index("ctx")
    tp = lax.axis_index("tp")
    me = ctx * n_tp + tp
    x_lo = ctx // n_tp
    z = lax.rem(ctx, n_tp) // 2
    core = lax.rem(ctx, 2)
    x_hi = tp // RING
    y = lax.rem(tp, RING)
    x = 2 * x_hi + x_lo
    pair = x_lo * RING + z
    mine = pair * 2 + x_hi
    slot = core * RING + y

    def at(x_at, z_at, y_at, core_at):
        return (lax.rem(x_at, 2) * n_tp + z_at * 2 + core_at, (x_at // 2) * RING + y_at)

    def along(step):
        other = lax.rem(me + step + n_dev, n_dev)
        return (other // n_tp, lax.rem(other, n_tp))

    def turn(value, step):
        return lax.rem(value + step + 2 * RING, RING)

    def y_dev(step):
        return at(x, z, turn(y, step), core)

    def group_dev(g):
        p = g // 2
        return at(2 * lax.rem(g, 2) + p // RING, lax.rem(p, RING), y, core)

    sibling = at(x, z, y, 1 - core)

    def remote(src, dst, send_sem, recv_sem, device):
        return pltpu.make_async_remote_copy(
            src_ref=src, dst_ref=dst, send_sem=send_sem, recv_sem=recv_sem,
            device_id=device, device_id_type=MESH,
        )

    barrier = pltpu.get_barrier_semaphore()

    def greet(device):
        pl.semaphore_signal(barrier, inc=1, device_id=device, device_id_type=MESH)

    for e in range(1, RING):
        greet(y_dev(e))
        greet(at(x, z, turn(y, e), 1 - core))
    greet(sibling)
    greet(along(-reach))
    greet(along(-1))

    def greet_plane(d, carry):
        greet(group_dev(lax.rem(mine + d, n_ctx)))
        return carry

    lax.fori_loop(1, n_ctx, greet_plane, 0)
    pl.semaphore_wait(barrier, 2 * RING + 1 + n_ctx - 1)

    def block_cols(hc):
        return lanes(hc * kv_chunk, kv_chunk)

    def halo_copy(which, hc, d, device, source):
        buf = (kbuf, vbuf)[which]
        return remote(
            buf.at[sublanes(source * rows, rows), block_cols(hc)],
            buf.at[pl.ds((reach - d) * rows, rows), block_cols(hc)],
            hs_sem.at[which, hc, d - 1],
            hr_sem.at[which, hc, d - 1],
            device,
        )

    def halo_far(which, hc):
        return halo_copy(which, hc, reach, along(reach), reach)

    def halo_near(which, hc, e):
        return halo_copy(which, hc, e, y_dev(e), jnp.where(y + e < RING, reach, 0))

    kbuf[reach * rows :, :] = k_ref[...]
    vbuf[reach * rows :, :] = v_ref[...]
    for hc in range(CHUNKS):
        for which in range(2):
            halo_far(which, hc).start()

    is_home = core == x_hi

    def shard_parts(to):
        return (
            (wq_hbm, w_all.at[to, :, 0:q_width]),
            (wk_hbm, w_all.at[to, :, q_width : q_width + HEAD]),
            (wv_hbm, w_all.at[to, :, q_width + HEAD : q_width + 2 * HEAD]),
            (wo_hbm, wo_all.at[to]),
        )

    def hand_over(i):
        src, dst = shard_parts(ctx)[i]
        return remote(src, dst, ho_sem.at[0, i], ho_sem.at[1, i], sibling)

    def hand_over_arrival(i):
        src, dst = shard_parts(ctx + 1 - 2 * core)[i]
        return remote(src, dst, ho_sem.at[0, i], ho_sem.at[1, i], sibling)

    def stay(i):
        src, dst = shard_parts(ctx)[i]
        return pltpu.make_async_copy(src, dst, ho_sem.at[2, i])

    @pl.when(is_home)
    def _():
        for i in range(4):
            stay(i).start()

    @pl.when(jnp.logical_not(is_home))
    def _():
        for i in range(4):
            hand_over(i).start()

    for hc in range(CHUNKS):
        for which in range(2):
            for e in range(1, RING):

                @pl.when(y + e < RING)
                def _():
                    halo_near(which, hc, e).start()

    def offsets(src):
        off_x = turn(x, -2 * core - src // n_tp)
        off_z = turn(z, -(lax.rem(src, n_tp) // 2))
        return off_x, off_z, lax.rem(src, 2)

    def hop(kind, path, src, lane):
        buf = (w_all, wo_all)[kind]
        piece = buf.at[src, pl.ds(path * half, half), :]
        device = (
            at(turn(x, 1), z, y, core),
            at(turn(x, -1), z, y, core),
            at(x, turn(z, 1), y, core),
            at(x, turn(z, -1), y, core),
        )[lane]
        return remote(
            piece, piece, wgs_sem.at[kind, path, src, lane], wgr_sem.at[kind, path, src], device
        )

    def hop_wanted(path, src, lane):
        off_x, off_z, c = offsets(src)
        off = off_x if lane < 2 else off_z
        if lane % 2 == 0:
            wanted = (off == 0) | ((off == 1) & (c == 0))
        else:
            wanted = (off == 0) | ((off == 3) & (c == 1))
        if path == 0 and lane < 2:
            wanted = wanted & (off_z == 0)
        if path == 1 and lane >= 2:
            wanted = wanted & (off_x == 0)
        return wanted

    def launch(kind, path, src):
        for lane in range(4):

            @pl.when(hop_wanted(path, src, lane))
            def _():
                hop(kind, path, src, lane).start()

    def arrive(kind, path, src):
        hop(kind, path, src, 0).wait_recv()
        launch(kind, path, src)

    def settle(kind):
        def one(src, carry):
            for path in range(2):
                for lane in range(4):

                    @pl.when(hop_wanted(path, src, lane))
                    def _():
                        hop(kind, path, src, lane).wait_send()

            return carry

        lax.fori_loop(0, n_ctx, one, 0)

    def origin(kind):
        @pl.when(is_home)
        def _():
            for i in range(4):
                if (i == 3) == (kind == 1):
                    stay(i).wait()
                    hand_over_arrival(i).wait_recv()
            for c in range(2):
                src = x_lo * n_tp + z * 2 + c
                launch(kind, 0, src)
                launch(kind, 1, src)

    def first_phase(kind):
        def one(i, carry):
            j, c = i // 2, lax.rem(i, 2)
            src = j * n_tp + z * 2 + c
            off_x, _, _ = offsets(src)

            @pl.when(off_x != 0)
            def _():
                arrive(kind, 0, src)

            return carry

        def two(i, carry):
            order, c = i // 2, lax.rem(i, 2)
            off = jnp.where(order == 0, 1, RING - order)
            arrive(kind, 1, x_lo * n_tp + turn(z, -off) * 2 + c)
            return carry

        lax.fori_loop(0, 4, one, 0)

        @pl.when(is_home)
        def _():
            lax.fori_loop(0, 6, two, 0)

    def second_phase(kind, step):
        off_first = jnp.where(step == 0, 1, RING - step)
        off_second = jnp.where(step < 2, step, 5 - step)

        def one(i, carry):
            j, c = i // 2, lax.rem(i, 2)

            @pl.when(step < 3)
            def _():
                arrive(kind, 0, j * n_tp + turn(z, -off_first) * 2 + c)

            src = j * n_tp + turn(z, -off_second) * 2 + c
            off_x, _, _ = offsets(src)

            @pl.when(off_x != 0)
            def _():
                arrive(kind, 1, src)

            return carry

        lax.fori_loop(0, 4, one, 0)

    origin(0)

    for hc in range(CHUNKS):
        for which in range(2):
            halo_far(which, hc).wait_recv()
        for which in range(2):
            for e in range(1, RING):

                @pl.when(y + e >= RING)
                def _():
                    halo_near(which, hc, e).start()

    q_at = lax.broadcasted_iota(jnp.int32, (rows, span), 0)
    l_at = lax.broadcasted_iota(jnp.int32, (rows, span), 1)
    gap = reach * rows + q_at - l_at
    outside = (gap < 0) | (l_at < (reach - me) * rows)
    dist[...] = jnp.where(outside, 2 * span, gap)
    ssq[...] = jnp.zeros_like(ssq)

    def a_rows(s):
        return sublanes(s * own, own)

    def a_piece(hc, s):
        return a_full.at[a_rows(s), lanes(hc * q_chunk, q_chunk)]

    def a_copy(hc, e):
        piece = a_piece(hc, slot)
        device = sibling if e == 0 else y_dev(e)
        return remote(piece, piece, as_sem.at[hc, e], ar_sem.at[hc, slot], device)

    def a_onward(hc, e):
        s = core * RING + turn(y, -e)
        piece = a_piece(hc, s)
        return remote(piece, piece, af_sem.at[hc, e], ar_sem.at[hc, s], sibling)

    def a_other(hc, y_at):
        s = (1 - core) * RING + y_at
        piece = a_piece(hc, s)
        return remote(piece, piece, af_sem.at[hc, 0], ar_sem.at[hc, s], sibling)

    part_heads = group // 2

    def chunk(hc, carry):
        for which in range(2):
            for e in range(1, RING):
                halo_near(which, hc, e).wait_recv()
        for u in range(kv_chunk // HEAD):
            kv_cols = lanes(hc * kv_chunk + u * HEAD, HEAD)
            keys = kbuf[:, kv_cols]
            values = vbuf[:, kv_cols]
            for part in range(2):
                first = (hc * (kv_chunk // HEAD) + u) * group + part * part_heads
                qs = jnp.concatenate(
                    [q_ref[:, lanes((first + i) * HEAD, HEAD)] for i in range(part_heads)], axis=0
                )
                scores = lax.dot_general(
                    qs, keys, (((1,), (1,)), ((), ())), preferred_element_type=F32
                )
                weights, totals = [], []
                for i in range(part_heads):
                    s = scores[i * rows : (i + 1) * rows] * (LOG2E * HEAD**-0.5)
                    s = jnp.where(dist[...] < win_ref[first + i], s, -1e30)
                    p = jnp.exp2(s - s.max(-1, keepdims=True))
                    totals.append(p.sum(-1, keepdims=True))
                    weights.append(p.astype(BF16))
                out = jnp.dot(
                    jnp.concatenate(weights, axis=0), values, preferred_element_type=F32
                )
                for i in range(part_heads):
                    cols = lanes((first + i) * HEAD, HEAD)
                    stream[first + i] = (
                        x_ref[:, cols].astype(F32) + out[i * rows : (i + 1) * rows] / totals[i]
                    )
        for i in range(q_chunk // HEAD):
            cols = lanes(hc * q_chunk + i * HEAD, HEAD)
            head = hc * (q_chunk // HEAD) + i
            pooled = sum(
                pw_ref[j : j + 1, cols] * stream[head, pl.ds(j, own, stride=POOL), :]
                for j in range(POOL)
            )
            pooled_v[:, cols] = pooled
            ssq[...] += pooled * pooled
            a_full[a_rows(slot), cols] = (pooled * gain_ref[:, cols]).astype(BF16)
        for e in range(RING):
            a_copy(hc, e).start()

        @pl.when(hc == 0)
        def _():
            first_phase(0)

        @pl.when(hc > 0)
        def _():
            second_phase(0, hc - 1)

        return carry

    lax.fori_loop(0, CHUNKS, chunk, 0)

    mean = ssq[...].sum(-1, keepdims=True) * (1.0 / width)
    rs_all[slot] = jnp.broadcast_to(lax.rsqrt(mean + 1e-05), ssq.shape)

    def rs_copy(e, other):
        device = at(x, z, turn(y, e), 1 - core if other else core)
        return remote(
            rs_all.at[slot], rs_all.at[slot], rss_sem.at[other, e], rsr_sem.at[slot], device
        )

    def rs_arrival(e, other):
        s = (1 - core if other else core) * RING + turn(y, e)
        return remote(
            rs_all.at[s], rs_all.at[s], rss_sem.at[other, e], rsr_sem.at[s], sibling
        )

    others = [(e, other) for other in range(2) for e in range(RING) if (e, other) != (0, 0)]
    for e, other in others:
        rs_copy(e, other).start()

    def a_relay(hc, carry):
        for e in range(1, RING):
            a_onward(hc, e).wait_recv()
            a_onward(hc, e).start()
        return carry

    lax.fori_loop(0, CHUNKS, a_relay, 0)
    second_phase(0, jnp.int32(3))

    def a_finish(hc, carry):
        for y_at in range(RING):
            a_other(hc, y_at).wait_recv()
        return carry

    lax.fori_loop(0, CHUNKS, a_finish, 0)
    for e, other in others:
        rs_arrival(e, other).wait_recv()
    origin(1)

    acc[...] = jnp.zeros_like(acc)

    def project(k, carry):
        acc[...] += jnp.dot(
            a_full[:, lanes(k * depth, depth)], w_all[k], preferred_element_type=F32
        )
        return carry

    lax.fori_loop(0, n_ctx, project, 0)
    row_scale = jnp.concatenate([rs_all[s] for s in range(n_tp)], axis=0)[:, 0:1]
    kv_all[mine] = (acc[:, q_width:] * row_scale).astype(BF16)

    def kv_copy(to):
        return remote(
            kv_all.at[mine], kv_all.at[mine], kvs_sem.at[to], kvr_sem.at[mine], group_dev(to)
        )

    def kv_arrival(source):
        return remote(
            kv_all.at[source], kv_all.at[source], kvs_sem.at[source], kvr_sem.at[source],
            group_dev(source),
        )

    partner = pair * 2 + 1 - x_hi

    def kv_send(to, carry):
        kv_copy(to).start()
        return carry

    kv_copy(partner).start()
    lax.fori_loop(pair * 2 + 2, n_ctx, kv_send, 0)
    for h in range(heads):
        q_all[h] = (acc[:, h * HEAD : (h + 1) * HEAD] * row_scale).astype(BF16)

    def attend(b, first):
        keys = jnp.concatenate([kv_all[2 * b, :, :HEAD], kv_all[2 * b + 1, :, :HEAD]], axis=0)
        values = jnp.concatenate([kv_all[2 * b, :, HEAD:], kv_all[2 * b + 1, :, HEAD:]], axis=0)
        for h in range(heads):
            s = lax.dot_general(
                q_all[h], keys, (((1,), (1,)), ((), ())), preferred_element_type=F32
            ) * (LOG2E * HEAD**-0.5)
            if first:
                run = all_rows // 2
                row = lax.broadcasted_iota(jnp.int32, s.shape, 0)
                col = lax.broadcasted_iota(jnp.int32, s.shape, 1)
                q_pos = row + x_hi * run + jnp.where(row >= run, run, 0)
                in_block = jnp.where(col >= all_rows, col - all_rows, col)
                k_pos = (
                    in_block + jnp.where(col >= all_rows, run, 0) + jnp.where(in_block >= run, run, 0)
                )
                s = jnp.where(k_pos <= q_pos, s, -1e30)
                new_top = s.max(-1, keepdims=True)
                p = jnp.exp2(s - new_top)
                total[h] = p.sum(-1, keepdims=True)
                mixed[h] = jnp.dot(p.astype(BF16), values, preferred_element_type=F32)
            else:
                old = top[h]
                new_top = jnp.maximum(old, s.max(-1, keepdims=True))
                scale = jnp.exp2(old - new_top)
                p = jnp.exp2(s - new_top)
                total[h] = total[h] * scale + p.sum(-1, keepdims=True)
                mixed[h] = mixed[h] * scale + jnp.dot(
                    p.astype(BF16), values, preferred_element_type=F32
                )
            top[h] = new_top

    kv_arrival(partner).wait_recv()
    attend(pair, True)

    def earlier(b, carry):
        @pl.when(b < pair)
        def _():
            kv_arrival(2 * b).wait_recv()
            kv_arrival(2 * b + 1).wait_recv()
            attend(b, False)

        @pl.when(b == 1)
        def _():
            first_phase(1)

        @pl.when((b >= 3) & (b < 7))
        def _():
            second_phase(1, b - 3)

        return carry

    lax.fori_loop(0, n_ctx // 2, earlier, 0)
    for h in range(heads):
        heads_v[:, h * HEAD : (h + 1) * HEAD] = (mixed[h] / total[h]).astype(BF16)

    per = n_ctx // GROUPS
    cols_out = wo_all.shape[2]
    wide = per * cols_out

    def s_copy(g):
        where = lanes(g * wide, wide)
        return remote(s_send.at[:, where], s_got.at[:, where], ss_sem.at[g], sr_sem.at[g], sibling)

    def multiply(g, carry):
        for i in range(per):
            b = g * per + i
            where = lanes(b * cols_out, cols_out)
            product = jnp.dot(heads_v[...], wo_all[b], preferred_element_type=F32)
            low, high = product[: all_rows // 2], product[all_rows // 2 :]
            keep[:, where] = jnp.where(core == 0, low, high).astype(BF16)
            s_send[:, where] = jnp.where(core == 0, high, low).astype(BF16)
        s_copy(g).start()
        return carry

    lax.fori_loop(0, GROUPS, multiply, 0)

    def y_copy(g, e):
        where = lanes(g * wide, wide)
        return remote(
            y_send.at[a_rows(turn(y, e)), where], y_got.at[a_rows(y), where],
            ys_sem.at[g, e], yr_sem.at[g, y], y_dev(e),
        )

    def y_arrival(g, e):
        where = lanes(g * wide, wide)
        source = turn(y, e)
        return remote(
            y_send.at[a_rows(source), where], y_got.at[a_rows(source), where],
            ys_sem.at[g, e], yr_sem.at[g, source], y_dev(e),
        )

    def reduce_cores(g, carry):
        where = lanes(g * wide, wide)
        s_copy(g).wait_recv()
        y_send[:, where] = (keep[:, where].astype(F32) + s_got[:, where].astype(F32)).astype(BF16)
        for e in range(1, RING):
            y_copy(g, e).start()
        pooled_v[:, where] += (
            keep[a_rows(y), where].astype(F32) + s_got[a_rows(y), where].astype(F32)
        )
        return carry

    lax.fori_loop(0, GROUPS, reduce_cores, 0)

    def reduce_ring(g, carry):
        where = lanes(g * wide, wide)
        for e in range(1, RING):
            y_arrival(g, e).wait_recv()
        value = pooled_v[:, where]
        for e in range(1, RING):
            value += y_got[a_rows(turn(y, e)), where].astype(F32)
        pooled_v[:, where] = value
        return carry

    lax.fori_loop(0, GROUPS, reduce_ring, 0)

    piece = last_send.shape[1]
    for i in range(last_send.shape[0]):
        last_send[i : i + 1, :] = pooled_v[own - 1 : own, i * piece : (i + 1) * piece]
    last = remote(last_send, last_got, l_sem.at[0], l_sem.at[1], along(1))
    last.start()
    shifted[1:own, :] = pooled_v[0 : own - 1, :]
    last.wait()
    first_row = jnp.where(me == 0, 0.0, last_got[...])
    for i in range(last_send.shape[0]):
        shifted[0:1, i * piece : (i + 1) * piece] = first_row[i : i + 1, :]

    def result(h):
        return pltpu.make_async_copy(
            stream.at[h], out_hbm.at[:, lanes(h * HEAD, HEAD)], o_sem.at[h]
        )

    def combine(i, carry):
        for u in range(group):
            h = i * group + u
            cols = lanes(h * HEAD, HEAD)
            add = shifted[:, cols]
            for j in range(POOL):
                where = pl.ds(j, own, stride=POOL)
                stream[h, where, :] = stream[h, where, :] + up_ref[j : j + 1, cols] * add
            result(h).start()
        return carry

    lax.fori_loop(0, width // HEAD // group, combine, 0)

    for hc in range(CHUNKS):
        for which in range(2):
            halo_far(which, hc).wait_send()
            for e in range(1, RING):
                halo_near(which, hc, e).wait_send()

    @pl.when(jnp.logical_not(is_home))
    def _():
        for i in range(4):
            hand_over(i).wait_send()

    settle(0)
    settle(1)

    def a_settle(hc, carry):
        for e in range(RING):
            a_copy(hc, e).wait_send()
        for e in range(1, RING):
            a_onward(hc, e).wait_send()
        return carry

    lax.fori_loop(0, CHUNKS, a_settle, 0)
    for e, other in others:
        rs_copy(e, other).wait_send()

    def kv_settle(to, carry):
        kv_copy(to).wait_send()
        return carry

    kv_copy(partner).wait_send()
    lax.fori_loop(pair * 2 + 2, n_ctx, kv_settle, 0)

    def sums_settle(g, carry):
        s_copy(g).wait_send()
        for e in range(1, RING):
            y_copy(g, e).wait_send()
        return carry

    lax.fori_loop(0, GROUPS, sums_settle, 0)

    def out_settle(h, carry):
        result(h).wait()
        return carry

    lax.fori_loop(0, width // HEAD, out_settle, 0)


def per_device(
    mesh, fine_x, fine_q, fine_k, fine_v, windows, pool_w, norm_gain, w_query, w_key, w_value, w_out, up_w
):
    rows, width = fine_q.shape
    kv_width = fine_k.shape[1]
    n_tp, n_ctx = mesh.shape["tp"], mesh.shape["ctx"]
    reach = WIN // rows
    span = (reach + 1) * rows
    own = rows // POOL
    all_rows = own * n_tp
    depth, q_width = w_query.shape
    heads = q_width // HEAD
    w_cols = q_width + 2 * HEAD
    dma = pltpu.SemaphoreType.DMA
    return pl.pallas_call(
        block_kernel,
        out_shape=jax.ShapeDtypeStruct((rows, width), F32),
        in_specs=[VMEM_SPEC] * 4
        + [pl.BlockSpec(memory_space=pltpu.SMEM)]
        + [VMEM_SPEC] * 3
        + [ANY_SPEC] * 4,
        out_specs=ANY_SPEC,
        scratch_shapes=[
            pltpu.VMEM((span, kv_width), BF16),
            pltpu.VMEM((span, kv_width), BF16),
            pltpu.VMEM((rows, span), jnp.int32),
            pltpu.VMEM((width // HEAD, rows, HEAD), F32),
            pltpu.VMEM((own, width), F32),
            pltpu.VMEM((all_rows, width), BF16),
            pltpu.VMEM((n_tp, own, HEAD), F32),
            pltpu.VMEM((own, HEAD), F32),
            pltpu.VMEM((n_ctx, depth, w_cols), BF16),
            pltpu.VMEM((n_ctx,) + w_out.shape, BF16),
            pltpu.VMEM((all_rows, w_cols), F32),
            pltpu.VMEM((n_ctx, all_rows, 2 * HEAD), BF16),
            pltpu.VMEM((heads, all_rows, HEAD), BF16),
            pltpu.VMEM((heads, all_rows, 1), F32),
            pltpu.VMEM((heads, all_rows, 1), F32),
            pltpu.VMEM((heads, all_rows, HEAD), F32),
            pltpu.VMEM((all_rows, q_width), BF16),
            pltpu.VMEM((all_rows // 2, width), BF16),
            pltpu.VMEM((all_rows // 2, width), BF16),
            pltpu.VMEM((all_rows // 2, width), BF16),
            pltpu.VMEM((all_rows // 2, width), BF16),
            pltpu.VMEM((all_rows // 2, width), BF16),
            pltpu.VMEM((own, width), F32),
            pltpu.VMEM((8, width // 8), F32),
            pltpu.VMEM((8, width // 8), F32),
            dma((2, CHUNKS, reach)),
            dma((2, CHUNKS, reach)),
            dma((CHUNKS, RING)),
            dma((CHUNKS, n_tp)),
            dma((CHUNKS, RING)),
            dma((2, RING)),
            dma((n_tp,)),
            dma((3, 4)),
            dma((2, 2, n_ctx, 4)),
            dma((2, 2, n_ctx)),
            dma((n_ctx,)),
            dma((n_ctx,)),
            dma((GROUPS,)),
            dma((GROUPS,)),
            dma((GROUPS, RING)),
            dma((GROUPS, RING)),
            dma((2,)),
            dma((width // HEAD,)),
        ],
        compiler_params=pltpu.CompilerParams(
            collective_id=0, has_side_effects=True, vmem_limit_bytes=62 * 2**20
        ),
        name="hourglass",
    )(
        fine_q, fine_k, fine_v, fine_x, windows, pool_w, norm_gain[None], up_w,
        w_query, w_key, w_value, w_out,
    )


def solution(mesh):
    placed = (
        P(("ctx", "tp"), None),
        P(("ctx", "tp"), None),
        P(("ctx", "tp"), None),
        P(("ctx", "tp"), None),
        P(),
        P(),
        P(),
        P("ctx", "tp"),
        P("ctx", "tp"),
        P("ctx", "tp"),
        P("tp", "ctx"),
        P(),
    )
    return jax.shard_map(
        functools.partial(per_device, mesh),
        mesh=mesh,
        in_specs=placed,
        out_specs=P(("ctx", "tp"), None),
        check_vma=False,
    )
```

time: 596 us -> 272 us (0.46)
  waiting for transfers between devices: 419 us -> 0 us
  Pallas kernels: 0 us -> 268 us
  matrix products: 66.7 us -> 0 us
  other arithmetic: 34.3 us -> 0 us
  local copies, waits for them, and re-layouts: 35.8 us -> 4.61 us
  starting transfers between devices: 20.5 us -> 0 us
  between operations: 13.7 us -> 0.01 us
    all_gather x7 -> x0, waiting for transfers between devices: 318 us -> none  [the longest x1 122 us: per_device(): block_f = lax.all_gather(pooled, 'tp', axis=0, tiled=True)]
    pallas_call x0 -> x1, Pallas kernels: none -> 268 us  [per_device(): pl.pallas_call(block_kernel, out_shape=jax.ShapeDtypeStruct((rows, width)...]
    reduce_scatter x1 -> x0, waiting for transfers between devices: 85.5 us -> none  [per_device(): lax.psum_scatter(jnp.dot(head_out, out_full, preferred_element_type=jnp.f...]
    dot_general x7 -> x0, matrix products: 47 us -> none  [the longest x1 10.4 us: per_device(): jnp.einsum('kgql,lkd->qkgd', weights.astype(jnp.bfloat16), value_piece.re...]
    ppermute x5 -> x0, starting transfers between devices: 20.2 us -> none  [passed_along(): return lax.ppermute(block, axis, route)]
    sub x1 -> x0, matrix products: 19.7 us -> none  [attend_window(): weights = jnp.where(allowed, jnp.exp(scores - row_top), 0.0)]
    reduce_sum x3 -> x0, other arithmetic: 14.4 us -> none  [the longest x1 6.03 us: per_device(): (stream.reshape(pool_rows, POOL, model_width) * pool_w[None]).sum(1)]
    ppermute x5 -> x0, waiting for transfers between devices: 12.9 us -> none  [passed_along(): return lax.ppermute(block, axis, route)]
  transfers between devices with their start and end apart: 13 -> 0, of which waited for: 11 -> 0; matrix products, arithmetic and copies ran while one was open for 9% -> 0% of each run, Pallas kernels for 0% -> 0%
where the time goes in v2:
time: 272 us
  Pallas kernels  268 us (99%)
  local copies, waits for them, and re-layouts  4.61 us (2%)
    pallas_call x1, Pallas kernels, per_device(): pl.pallas_call(block_kernel, out_shape=jax.ShapeDtypeStruct((rows, width)...  268 us

profile of v2, /device:TPU:0, one launch (start us, length us, event | category | flops | bytes accessed | tf_op | source)
XLA Modules:
  0.0 272.2 jit_solution(18272383847424895710)
XLA Ops:
  0.0 267.6 %hourglass.1 = f32[128,8192]{1,0:T(8,128)} custom-call(bf16[128,8192]{1,0:T(8,128)(2,1)} %q_ref.1, bf16[128,1024]{1,0:T(8,128)(2,1)} %k_ref.1, bf16[128,1024]{1,0:T(8,128)(2,1)} %v_ref.1, bf16[128,8192]{1,0:T(8,128)(2,1)} %x_ref.1, s32[64]{0:T(128)} %win_ref.1, f32[4,8192]{1,0:T(4,128)} %pw_ref.1, f32[1,8192]{1,0:T(1,128)} %bitcast.1, f32[4,8192]{1,0:T(4,128)} %up_ref.1, ...), custom_call_target="tpu_custom_call" | custom-call | tf_op jit(solution)/shard_map/hourglass/pallas_call | solution.py:671
  267.6 4.6 %copy.14 = f32[128,8192]{1,0:T(8,128)} copy(f32[128,8192]{1,0:T(8,128)} %hourglass.1) | data formatting | bytes 8388608

commit v3 on v2

--- a/solution.py
+++ b/solution.py
@@ -18,7 +18,7 @@
 VMEM_SPEC = pl.BlockSpec(memory_space=pltpu.VMEM)
 ANY_SPEC = pl.BlockSpec(memory_space=pl.ANY)
 CHUNKS = 4
-GROUPS = 8
+SLOTS = 4
 
 
 def lanes(start, size):
@@ -32,12 +32,12 @@
 def block_kernel(
     q_ref, k_ref, v_ref, x_ref, win_ref, pw_ref, gain_ref, up_ref, wq_hbm, wk_hbm, wv_hbm, wo_hbm,
     out_hbm,
-    kbuf, vbuf, dist, stream, pooled_v, a_full, rs_all, ssq,
-    w_all, wo_all, acc, kv_all, q_all, top, total, mixed, heads_v,
-    keep, s_send, s_got, y_send, y_got, shifted, last_send, last_got,
-    hs_sem, hr_sem, as_sem, ar_sem, af_sem, rss_sem, rsr_sem,
-    ho_sem, wgs_sem, wgr_sem, kvs_sem, kvr_sem,
-    ss_sem, sr_sem, ys_sem, yr_sem, l_sem, o_sem,
+    kbuf, vbuf, dist, stream, pooled_v, a_own, a_full, rs_all, ssq,
+    w_all, wo_all, kv_part, q_part, kv_got, q_got, kv_all, q_all, top, total, mixed, h_all,
+    keep, s_send, s_got, y_send, y_got, ring_sum, z_send, z_got, shifted, last_send, last_got,
+    hs_sem, hr_sem, azs_sem, azr_sem, ays_sem, ayr_sem, acs_sem, rss_sem, rsr_sem,
+    ho_sem, wgs_sem, wgr_sem, ps_sem, pr_sem, kvs_sem, kvr_sem, hzs_sem, hzr_sem,
+    ss_sem, sr_sem, ys_sem, yr_sem, zs_sem, zr_sem, l_sem, o_sem,
 ):
     rows, width = q_ref.shape
     kv_width = k_ref.shape[1]
@@ -47,13 +47,12 @@
     own = rows // POOL
     kv_chunk = kv_width // CHUNKS
     q_chunk = width // CHUNKS
-    n_ctx = w_all.shape[0]
-    depth = w_all.shape[1]
-    half = depth // 2
-    q_width = heads_v.shape[1]
+    depth = w_all.shape[0] // SLOTS
+    q_width = h_all.shape[2]
     heads = q_width // HEAD
-    all_rows = heads_v.shape[0]
+    all_rows = h_all.shape[1]
     n_tp = 2 * RING
+    n_ctx = 4 * RING
     n_dev = n_ctx * n_tp
 
     ctx = lax.axis_index("ctx")
@@ -82,6 +81,9 @@
     def y_dev(step):
         return at(x, z, turn(y, step), core)
 
+    def z_dev(step):
+        return at(x, turn(z, step), y, core)
+
     def group_dev(g):
         p = g // 2
         return at(2 * lax.rem(g, 2) + p // RING, lax.rem(p, RING), y, core)
@@ -140,24 +142,26 @@
 
     is_home = core == x_hi
 
-    def shard_parts(to):
+    def shard_parts(core_at):
+        to = x_lo * 2 + core_at
+        rows_to = sublanes(to * depth, depth)
         return (
-            (wq_hbm, w_all.at[to, :, 0:q_width]),
-            (wk_hbm, w_all.at[to, :, q_width : q_width + HEAD]),
-            (wv_hbm, w_all.at[to, :, q_width + HEAD : q_width + 2 * HEAD]),
+            (wq_hbm, w_all.at[rows_to, 0:q_width]),
+            (wk_hbm, w_all.at[rows_to, q_width : q_width + HEAD]),
+            (wv_hbm, w_all.at[rows_to, q_width + HEAD : q_width + 2 * HEAD]),
             (wo_hbm, wo_all.at[to]),
         )
 
     def hand_over(i):
-        src, dst = shard_parts(ctx)[i]
+        src, dst = shard_parts(core)[i]
         return remote(src, dst, ho_sem.at[0, i], ho_sem.at[1, i], sibling)
 
     def hand_over_arrival(i):
-        src, dst = shard_parts(ctx + 1 - 2 * core)[i]
+        src, dst = shard_parts(1 - core)[i]
         return remote(src, dst, ho_sem.at[0, i], ho_sem.at[1, i], sibling)
 
     def stay(i):
-        src, dst = shard_parts(ctx)[i]
+        src, dst = shard_parts(core)[i]
         return pltpu.make_async_copy(src, dst, ho_sem.at[2, i])
 
     @pl.when(is_home)
@@ -178,60 +182,25 @@
                 def _():
                     halo_near(which, hc, e).start()
 
-    def offsets(src):
-        off_x = turn(x, -2 * core - src // n_tp)
-        off_z = turn(z, -(lax.rem(src, n_tp) // 2))
-        return off_x, off_z, lax.rem(src, 2)
-
-    def hop(kind, path, src, lane):
-        buf = (w_all, wo_all)[kind]
-        piece = buf.at[src, pl.ds(path * half, half), :]
-        device = (
-            at(turn(x, 1), z, y, core),
-            at(turn(x, -1), z, y, core),
-            at(x, turn(z, 1), y, core),
-            at(x, turn(z, -1), y, core),
-        )[lane]
-        return remote(
-            piece, piece, wgs_sem.at[kind, path, src, lane], wgr_sem.at[kind, path, src], device
-        )
-
-    def hop_wanted(path, src, lane):
-        off_x, off_z, c = offsets(src)
-        off = off_x if lane < 2 else off_z
-        if lane % 2 == 0:
-            wanted = (off == 0) | ((off == 1) & (c == 0))
-        else:
-            wanted = (off == 0) | ((off == 3) & (c == 1))
-        if path == 0 and lane < 2:
-            wanted = wanted & (off_z == 0)
-        if path == 1 and lane >= 2:
-            wanted = wanted & (off_x == 0)
-        return wanted
-
-    def launch(kind, path, src):
-        for lane in range(4):
-
-            @pl.when(hop_wanted(path, src, lane))
+    def hop(kind, k, lane):
+        piece = w_all.at[sublanes(k * depth, depth)] if kind == 0 else wo_all.at[k]
+        device = at(turn(x, 1 if lane == 0 else -1), z, y, core)
+        return remote(piece, piece, wgs_sem.at[kind, k, lane], wgr_sem.at[kind, k], device)
+
+    def off_x(k):
+        return turn(x, -2 * core - k // 2)
+
+    def hop_wanted(k, lane):
+        onward = (off_x(k) == 1) & (lax.rem(k, 2) == 0)
+        back = (off_x(k) == 3) & (lax.rem(k, 2) == 1)
+        return (off_x(k) == 0) | (onward if lane == 0 else back)
+
+    def launch(kind, k):
+        for lane in range(2):
+
+            @pl.when(hop_wanted(k, lane))
             def _():
-                hop(kind, path, src, lane).start()
-
-    def arrive(kind, path, src):
-        hop(kind, path, src, 0).wait_recv()
-        launch(kind, path, src)
-
-    def settle(kind):
-        def one(src, carry):
-            for path in range(2):
-                for lane in range(4):
-
-                    @pl.when(hop_wanted(path, src, lane))
-                    def _():
-                        hop(kind, path, src, lane).wait_send()
-
-            return carry
-
-        lax.fori_loop(0, n_ctx, one, 0)
+                hop(kind, k, lane).start()
 
     def origin(kind):
         @pl.when(is_home)
@@ -241,55 +210,40 @@
                     stay(i).wait()
                     hand_over_arrival(i).wait_recv()
             for c in range(2):
-                src = x_lo * n_tp + z * 2 + c
-                launch(kind, 0, src)
-                launch(kind, 1, src)
-
-    def first_phase(kind):
-        def one(i, carry):
-            j, c = i // 2, lax.rem(i, 2)
-            src = j * n_tp + z * 2 + c
-            off_x, _, _ = offsets(src)
-
-            @pl.when(off_x != 0)
+                launch(kind, x_lo * 2 + c)
+
+    def relay(kind):
+        def one(k, carry):
+            @pl.when((off_x(k) == 1) | (off_x(k) == 3))
             def _():
-                arrive(kind, 0, src)
+                hop(kind, k, 0).wait_recv()
+                launch(kind, k)
 
             return carry
 
-        def two(i, carry):
-            order, c = i // 2, lax.rem(i, 2)
-            off = jnp.where(order == 0, 1, RING - order)
-            arrive(kind, 1, x_lo * n_tp + turn(z, -off) * 2 + c)
+        lax.fori_loop(0, SLOTS, one, 0)
+
+    def finish(kind):
+        def one(k, carry):
+            @pl.when(off_x(k) == 2)
+            def _():
+                hop(kind, k, 0).wait_recv()
+
             return carry
 
-        lax.fori_loop(0, 4, one, 0)
-
-        @pl.when(is_home)
-        def _():
-            lax.fori_loop(0, 6, two, 0)
-
-    def second_phase(kind, step):
-        off_first = jnp.where(step == 0, 1, RING - step)
-        off_second = jnp.where(step < 2, step, 5 - step)
-
-        def one(i, carry):
-            j, c = i // 2, lax.rem(i, 2)
-
-            @pl.when(step < 3)
-            def _():
-                arrive(kind, 0, j * n_tp + turn(z, -off_first) * 2 + c)
-
-            src = j * n_tp + turn(z, -off_second) * 2 + c
-            off_x, _, _ = offsets(src)
-
-            @pl.when(off_x != 0)
-            def _():
-                arrive(kind, 1, src)
+        lax.fori_loop(0, SLOTS, one, 0)
+
+    def settle(kind):
+        def one(k, carry):
+            for lane in range(2):
+
+                @pl.when(hop_wanted(k, lane))
+                def _():
+                    hop(kind, k, lane).wait_send()
 
             return carry
 
-        lax.fori_loop(0, 4, one, 0)
+        lax.fori_loop(0, SLOTS, one, 0)
 
     origin(0)
 
@@ -313,23 +267,46 @@
     def a_rows(s):
         return sublanes(s * own, own)
 
-    def a_piece(hc, s):
-        return a_full.at[a_rows(s), lanes(hc * q_chunk, q_chunk)]
-
-    def a_copy(hc, e):
-        piece = a_piece(hc, slot)
+    piece_cols = q_chunk // 2
+    block_rows = RING * own
+
+    def a_z_copy(hc, p):
+        to = lax.rem(hc, 2) * 2 + p
+        return remote(
+            a_own.at[:, lanes(hc * q_chunk + p * piece_cols, piece_cols)],
+            a_full.at[a_rows(slot * RING + z), lanes((hc // 2) * piece_cols, piece_cols)],
+            azs_sem.at[hc, p],
+            azr_sem.at[hc // 2, z],
+            at(x, to, y, core),
+        )
+
+    def a_z_arrival(j, e):
+        source = turn(z, e)
+        piece = a_full.at[a_rows(slot * RING + source), lanes(j * piece_cols, piece_cols)]
+        return remote(piece, piece, azs_sem.at[0, 0], azr_sem.at[j, source], z_dev(e))
+
+    def a_block(j, s):
+        return a_full.at[sublanes(s * block_rows, block_rows), lanes(j * piece_cols, piece_cols)]
+
+    def a_copy(j, e):
         device = sibling if e == 0 else y_dev(e)
-        return remote(piece, piece, as_sem.at[hc, e], ar_sem.at[hc, slot], device)
-
-    def a_onward(hc, e):
+        return remote(
+            a_block(j, slot), a_block(j, slot), ays_sem.at[j, e], ayr_sem.at[j, slot], device
+        )
+
+    def a_onward(j, e):
         s = core * RING + turn(y, -e)
-        piece = a_piece(hc, s)
-        return remote(piece, piece, af_sem.at[hc, e], ar_sem.at[hc, s], sibling)
-
-    def a_other(hc, y_at):
+        return remote(a_block(j, s), a_block(j, s), acs_sem.at[j, e], ayr_sem.at[j, s], sibling)
+
+    def a_other(j, y_at):
         s = (1 - core) * RING + y_at
-        piece = a_piece(hc, s)
-        return remote(piece, piece, af_sem.at[hc, 0], ar_sem.at[hc, s], sibling)
+        return remote(a_block(j, s), a_block(j, s), acs_sem.at[j, 0], ayr_sem.at[j, s], sibling)
+
+    def a_relay(j):
+        for e in range(1, RING):
+            a_z_arrival(j, e).wait_recv()
+        for e in range(RING):
+            a_copy(j, e).start()
 
     part_heads = group // 2
 
@@ -373,17 +350,32 @@
             )
             pooled_v[:, cols] = pooled
             ssq[...] += pooled * pooled
-            a_full[a_rows(slot), cols] = (pooled * gain_ref[:, cols]).astype(BF16)
-        for e in range(RING):
-            a_copy(hc, e).start()
-
-        @pl.when(hc == 0)
+            a_own[:, cols] = (pooled * gain_ref[:, cols]).astype(BF16)
+        for p in range(2):
+            to = lax.rem(hc, 2) * 2 + p
+
+            @pl.when(to != z)
+            def _():
+                a_z_copy(hc, p).start()
+
+            @pl.when(to == z)
+            def _():
+                a_full[a_rows(slot * RING + z), lanes((hc // 2) * piece_cols, piece_cols)] = a_own[
+                    :, lanes(hc * q_chunk + p * piece_cols, piece_cols)
+                ]
+
+        @pl.when(hc == 1)
         def _():
-            first_phase(0)
-
-        @pl.when(hc > 0)
+            relay(0)
+            origin(1)
+
+        @pl.when(hc == 2)
         def _():
-            second_phase(0, hc - 1)
+            a_relay(0)
+
+        @pl.when(hc == 3)
+        def _():
+            relay(1)
 
         return carry
 
@@ -408,36 +400,61 @@
     for e, other in others:
         rs_copy(e, other).start()
 
-    def a_relay(hc, carry):
-        for e in range(1, RING):
-            a_onward(hc, e).wait_recv()
-            a_onward(hc, e).start()
-        return carry
-
-    lax.fori_loop(0, CHUNKS, a_relay, 0)
-    second_phase(0, jnp.int32(3))
-
-    def a_finish(hc, carry):
+    a_relay(1)
+    for j in range(2):
+        for e in range(1, RING):
+            a_onward(j, e).wait_recv()
+            a_onward(j, e).start()
+    finish(0)
+    for j in range(2):
         for y_at in range(RING):
-            a_other(hc, y_at).wait_recv()
-        return carry
-
-    lax.fori_loop(0, CHUNKS, a_finish, 0)
+            a_other(j, y_at).wait_recv()
     for e, other in others:
         rs_arrival(e, other).wait_recv()
-    origin(1)
-
-    acc[...] = jnp.zeros_like(acc)
-
-    def project(k, carry):
-        acc[...] += jnp.dot(
-            a_full[:, lanes(k * depth, depth)], w_all[k], preferred_element_type=F32
-        )
-        return carry
-
-    lax.fori_loop(0, n_ctx, project, 0)
+
+    def part_copy(kind, e):
+        part, got = ((kv_part, kv_got), (q_part, q_got))[kind]
+        return remote(
+            part.at[turn(z, e)], got.at[z], ps_sem.at[kind, e], pr_sem.at[kind, z], z_dev(e)
+        )
+
+    def part_arrival(kind, e):
+        part, got = ((kv_part, kv_got), (q_part, q_got))[kind]
+        source = turn(z, e)
+        return remote(
+            part.at[source], got.at[source], ps_sem.at[kind, e], pr_sem.at[kind, source], z_dev(e)
+        )
+
+    def project(kind):
+        part = (kv_part, q_part)[kind]
+        cols = (slice(q_width, None), slice(0, q_width))[kind]
+
+        def one(m, carry):
+            product = jnp.dot(
+                a_full[sublanes(m * all_rows, all_rows), :], w_all[:, cols], preferred_element_type=F32
+            ).astype(BF16)
+            for i in range(2):
+                for zz in range(RING):
+                    first = (i * RING + zz) * own
+                    part[zz, a_rows(m * 2 + i), :] = product[first : first + own]
+            return carry
+
+        lax.fori_loop(0, RING, one, 0)
+        for e in range(1, RING):
+            part_copy(kind, e).start()
+
+    def part_sum(kind):
+        part, got = ((kv_part, kv_got), (q_part, q_got))[kind]
+        value = part[z].astype(F32)
+        for e in range(1, RING):
+            part_arrival(kind, e).wait_recv()
+            value += got[turn(z, e)].astype(F32)
+        return value
+
+    project(0)
+    project(1)
     row_scale = jnp.concatenate([rs_all[s] for s in range(n_tp)], axis=0)[:, 0:1]
-    kv_all[mine] = (acc[:, q_width:] * row_scale).astype(BF16)
+    kv_all[mine] = (part_sum(0) * row_scale).astype(BF16)
 
     def kv_copy(to):
         return remote(
@@ -458,8 +475,9 @@
 
     kv_copy(partner).start()
     lax.fori_loop(pair * 2 + 2, n_ctx, kv_send, 0)
+    q_rows = (part_sum(1) * row_scale).astype(BF16)
     for h in range(heads):
-        q_all[h] = (acc[:, h * HEAD : (h + 1) * HEAD] * row_scale).astype(BF16)
+        q_all[h] = q_rows[:, h * HEAD : (h + 1) * HEAD]
 
     def attend(b, first):
         keys = jnp.concatenate([kv_all[2 * b, :, :HEAD], kv_all[2 * b + 1, :, :HEAD]], axis=0)
@@ -497,86 +515,122 @@
     attend(pair, True)
 
     def earlier(b, carry):
-        @pl.when(b < pair)
-        def _():
-            kv_arrival(2 * b).wait_recv()
-            kv_arrival(2 * b + 1).wait_recv()
-            attend(b, False)
-
-        @pl.when(b == 1)
-        def _():
-            first_phase(1)
-
-        @pl.when((b >= 3) & (b < 7))
-        def _():
-            second_phase(1, b - 3)
-
-        return carry
-
-    lax.fori_loop(0, n_ctx // 2, earlier, 0)
+        kv_arrival(2 * b).wait_recv()
+        kv_arrival(2 * b + 1).wait_recv()
+        attend(b, False)
+        return carry
+
+    lax.fori_loop(0, pair, earlier, 0)
     for h in range(heads):
-        heads_v[:, h * HEAD : (h + 1) * HEAD] = (mixed[h] / total[h]).astype(BF16)
-
-    per = n_ctx // GROUPS
+        h_all[z, :, h * HEAD : (h + 1) * HEAD] = (mixed[h] / total[h]).astype(BF16)
+
+    def h_copy(e):
+        return remote(h_all.at[z], h_all.at[z], hzs_sem.at[e], hzr_sem.at[z], z_dev(e))
+
+    def h_arrival(e):
+        source = turn(z, e)
+        return remote(h_all.at[source], h_all.at[source], hzs_sem.at[e], hzr_sem.at[source], z_dev(e))
+
+    for e in range(1, RING):
+        h_copy(e).start()
+    finish(1)
+    for e in range(1, RING):
+        h_arrival(e).wait_recv()
+
     cols_out = wo_all.shape[2]
-    wide = per * cols_out
+
+    def out_cols(g):
+        return lanes(g * cols_out, cols_out)
 
     def s_copy(g):
-        where = lanes(g * wide, wide)
-        return remote(s_send.at[:, where], s_got.at[:, where], ss_sem.at[g], sr_sem.at[g], sibling)
+        return remote(
+            s_send.at[:, out_cols(g)], s_got.at[:, out_cols(g)], ss_sem.at[g], sr_sem.at[g], sibling
+        )
 
     def multiply(g, carry):
-        for i in range(per):
-            b = g * per + i
-            where = lanes(b * cols_out, cols_out)
-            product = jnp.dot(heads_v[...], wo_all[b], preferred_element_type=F32)
+        for zz in range(RING):
+            product = jnp.dot(h_all[zz], wo_all[g], preferred_element_type=F32)
             low, high = product[: all_rows // 2], product[all_rows // 2 :]
-            keep[:, where] = jnp.where(core == 0, low, high).astype(BF16)
-            s_send[:, where] = jnp.where(core == 0, high, low).astype(BF16)
+            stays = jnp.where(core == 0, low, high).astype(BF16)
+            goes = jnp.where(core == 0, high, low).astype(BF16)
+            for yy in range(RING):
+                at_rows = a_rows(yy * RING + zz)
+                keep[at_rows, out_cols(g)] = stays[yy * own : (yy + 1) * own]
+                s_send[at_rows, out_cols(g)] = goes[yy * own : (yy + 1) * own]
         s_copy(g).start()
         return carry
 
-    lax.fori_loop(0, GROUPS, multiply, 0)
+    lax.fori_loop(0, SLOTS, multiply, 0)
+
+    def y_rows(y_at):
+        return sublanes(y_at * block_rows, block_rows)
 
     def y_copy(g, e):
-        where = lanes(g * wide, wide)
-        return remote(
-            y_send.at[a_rows(turn(y, e)), where], y_got.at[a_rows(y), where],
+        return remote(
+            y_send.at[y_rows(turn(y, e)), out_cols(g)], y_got.at[y_rows(y), out_cols(g)],
             ys_sem.at[g, e], yr_sem.at[g, y], y_dev(e),
         )
 
     def y_arrival(g, e):
-        where = lanes(g * wide, wide)
         source = turn(y, e)
         return remote(
-            y_send.at[a_rows(source), where], y_got.at[a_rows(source), where],
+            y_send.at[y_rows(source), out_cols(g)], y_got.at[y_rows(source), out_cols(g)],
             ys_sem.at[g, e], yr_sem.at[g, source], y_dev(e),
         )
 
     def reduce_cores(g, carry):
-        where = lanes(g * wide, wide)
+        where = out_cols(g)
         s_copy(g).wait_recv()
         y_send[:, where] = (keep[:, where].astype(F32) + s_got[:, where].astype(F32)).astype(BF16)
         for e in range(1, RING):
             y_copy(g, e).start()
-        pooled_v[:, where] += (
-            keep[a_rows(y), where].astype(F32) + s_got[a_rows(y), where].astype(F32)
-        )
-        return carry
-
-    lax.fori_loop(0, GROUPS, reduce_cores, 0)
+        ring_sum[:, where] = (
+            keep[y_rows(y), where].astype(F32) + s_got[y_rows(y), where].astype(F32)
+        )
+        return carry
+
+    lax.fori_loop(0, SLOTS, reduce_cores, 0)
+
+    def z_copy(g, e):
+        return remote(
+            z_send.at[a_rows(turn(z, e)), out_cols(g)], z_got.at[a_rows(z), out_cols(g)],
+            zs_sem.at[g, e], zr_sem.at[g, z], z_dev(e),
+        )
+
+    def z_arrival(g, e):
+        source = turn(z, e)
+        return remote(
+            z_send.at[a_rows(source), out_cols(g)], z_got.at[a_rows(source), out_cols(g)],
+            zs_sem.at[g, e], zr_sem.at[g, source], z_dev(e),
+        )
+
+    def full_cols(g, z_at):
+        return lanes(((g // 2) * n_tp + z_at * 2 + lax.rem(g, 2)) * cols_out, cols_out)
 
     def reduce_ring(g, carry):
-        where = lanes(g * wide, wide)
+        where = out_cols(g)
         for e in range(1, RING):
             y_arrival(g, e).wait_recv()
-        value = pooled_v[:, where]
-        for e in range(1, RING):
-            value += y_got[a_rows(turn(y, e)), where].astype(F32)
-        pooled_v[:, where] = value
-        return carry
-
-    lax.fori_loop(0, GROUPS, reduce_ring, 0)
+        value = ring_sum[:, where]
+        for e in range(1, RING):
+            value += y_got[y_rows(turn(y, e)), where].astype(F32)
+        ring_sum[:, where] = value
+        z_send[:, where] = value.astype(BF16)
+        for e in range(1, RING):
+            z_copy(g, e).start()
+        pooled_v[:, full_cols(g, z)] += ring_sum[a_rows(z), where]
+        return carry
+
+    lax.fori_loop(0, SLOTS, reduce_ring, 0)
+
+    def take_home(g, carry):
+        for e in range(1, RING):
+            z_arrival(g, e).wait_recv()
+            source = turn(z, e)
+            pooled_v[:, full_cols(g, source)] += z_got[a_rows(source), out_cols(g)].astype(F32)
+        return carry
+
+    lax.fori_loop(0, SLOTS, take_home, 0)
 
     piece = last_send.shape[1]
     for i in range(last_send.shape[0]):
@@ -622,13 +676,24 @@
     settle(1)
 
     def a_settle(hc, carry):
+        for p in range(2):
+
+            @pl.when(lax.rem(hc, 2) * 2 + p != z)
+            def _():
+                a_z_copy(hc, p).wait_send()
+
+        return carry
+
+    lax.fori_loop(0, CHUNKS, a_settle, 0)
+    for j in range(2):
         for e in range(RING):
-            a_copy(hc, e).wait_send()
-        for e in range(1, RING):
-            a_onward(hc, e).wait_send()
-        return carry
-
-    lax.fori_loop(0, CHUNKS, a_settle, 0)
+            a_copy(j, e).wait_send()
+        for e in range(1, RING):
+            a_onward(j, e).wait_send()
+    for e in range(1, RING):
+        part_copy(0, e).wait_send()
+        part_copy(1, e).wait_send()
+        h_copy(e).wait_send()
     for e, other in others:
         rs_copy(e, other).wait_send()
 
@@ -643,9 +708,10 @@
         s_copy(g).wait_send()
         for e in range(1, RING):
             y_copy(g, e).wait_send()
-        return carry
-
-    lax.fori_loop(0, GROUPS, sums_settle, 0)
+            z_copy(g, e).wait_send()
+        return carry
+
+    lax.fori_loop(0, SLOTS, sums_settle, 0)
 
     def out_settle(h, carry):
         result(h).wait()
@@ -682,42 +748,55 @@
             pltpu.VMEM((rows, span), jnp.int32),
             pltpu.VMEM((width // HEAD, rows, HEAD), F32),
             pltpu.VMEM((own, width), F32),
-            pltpu.VMEM((all_rows, width), BF16),
+            pltpu.VMEM((own, width), BF16),
+            pltpu.VMEM((RING * all_rows, width // RING), BF16),
             pltpu.VMEM((n_tp, own, HEAD), F32),
             pltpu.VMEM((own, HEAD), F32),
-            pltpu.VMEM((n_ctx, depth, w_cols), BF16),
-            pltpu.VMEM((n_ctx,) + w_out.shape, BF16),
-            pltpu.VMEM((all_rows, w_cols), F32),
+            pltpu.VMEM((SLOTS * depth, w_cols), BF16),
+            pltpu.VMEM((SLOTS,) + w_out.shape, BF16),
+            pltpu.VMEM((RING, all_rows, 2 * HEAD), BF16),
+            pltpu.VMEM((RING, all_rows, q_width), BF16),
+            pltpu.VMEM((RING, all_rows, 2 * HEAD), BF16),
+            pltpu.VMEM((RING, all_rows, q_width), BF16),
             pltpu.VMEM((n_ctx, all_rows, 2 * HEAD), BF16),
             pltpu.VMEM((heads, all_rows, HEAD), BF16),
             pltpu.VMEM((heads, all_rows, 1), F32),
             pltpu.VMEM((heads, all_rows, 1), F32),
             pltpu.VMEM((heads, all_rows, HEAD), F32),
-            pltpu.VMEM((all_rows, q_width), BF16),
-            pltpu.VMEM((all_rows // 2, width), BF16),
-            pltpu.VMEM((all_rows // 2, width), BF16),
-            pltpu.VMEM((all_rows // 2, width), BF16),
-            pltpu.VMEM((all_rows // 2, width), BF16),
-            pltpu.VMEM((all_rows // 2, width), BF16),
+            pltpu.VMEM((RING, all_rows, q_width), BF16),
+        ]
+        + [pltpu.VMEM((RING * all_rows // 2, width // RING), BF16)] * 5
+        + [
+            pltpu.VMEM((RING * own, width // RING), F32),
+            pltpu.VMEM((RING * own, width // RING), BF16),
+            pltpu.VMEM((RING * own, width // RING), BF16),
             pltpu.VMEM((own, width), F32),
             pltpu.VMEM((8, width // 8), F32),
             pltpu.VMEM((8, width // 8), F32),
             dma((2, CHUNKS, reach)),
             dma((2, CHUNKS, reach)),
-            dma((CHUNKS, RING)),
-            dma((CHUNKS, n_tp)),
-            dma((CHUNKS, RING)),
+            dma((CHUNKS, 2)),
+            dma((2, RING)),
+            dma((2, RING)),
+            dma((2, n_tp)),
+            dma((2, RING)),
             dma((2, RING)),
             dma((n_tp,)),
             dma((3, 4)),
-            dma((2, 2, n_ctx, 4)),
-            dma((2, 2, n_ctx)),
+            dma((2, SLOTS, 2)),
+            dma((2, SLOTS)),
+            dma((2, RING)),
+            dma((2, RING)),
             dma((n_ctx,)),
             dma((n_ctx,)),
-            dma((GROUPS,)),
-            dma((GROUPS,)),
-            dma((GROUPS, RING)),
-            dma((GROUPS, RING)),
+            dma((RING,)),
+            dma((RING,)),
+            dma((SLOTS,)),
+            dma((SLOTS,)),
+            dma((SLOTS, RING)),
+            dma((SLOTS, RING)),
+            dma((SLOTS, RING)),
+            dma((SLOTS, RING)),
             dma((2,)),
             dma((width // HEAD,)),
         ],

time: 272 us -> 189 us (0.69)
  Pallas kernels: 268 us -> 183 us
    pallas_call x1, Pallas kernels: 268 us -> 183 us  [per_device(): pl.pallas_call(block_kernel, out_shape=jax.ShapeDtypeStruct((rows, width)...]
where the time goes in v3:
time: 189 us; the launch traced here: 188 us
  Pallas kernels  183 us (97%)
  local copies, waits for them, and re-layouts  4.61 us (2%)
    pallas_call x1, Pallas kernels, per_device(): pl.pallas_call(block_kernel, out_shape=jax.ShapeDtypeStruct((rows, width)...  183 us
    unnamed x1, local copies, waits for them, and re-layouts  4.61 us

profile of v3, /device:TPU:0, one launch (start us, length us, event | category | flops | bytes accessed | tf_op | source)
XLA Modules:
  0.0 187.7 jit_solution(1229148661763251051)
XLA Ops:
  0.0 183.1 %hourglass.1 = f32[128,8192]{1,0:T(8,128)} custom-call(bf16[128,8192]{1,0:T(8,128)(2,1)} %q_ref.1, bf16[128,1024]{1,0:T(8,128)(2,1)} %k_ref.1, bf16[128,1024]{1,0:T(8,128)(2,1)} %v_ref.1, bf16[128,8192]{1,0:T(8,128)(2,1)} %x_ref.1, s32[64]{0:T(128)} %win_ref.1, f32[4,8192]{1,0:T(4,128)} %pw_ref.1, f32[1,8192]{1,0:T(1,128)} %bitcast.1, f32[4,8192]{1,0:T(4,128)} %up_ref.1, ...), custom_call_target="tpu_custom_call" | custom-call | tf_op jit(solution)/shard_map/hourglass/pallas_call | solution.py:737
  183.1 4.6 %copy.14 = f32[128,8192]{1,0:T(8,128)} copy(f32[128,8192]{1,0:T(8,128)} %hourglass.1) | data formatting | bytes 8388608

commit v4 on v3

--- a/solution.py
+++ b/solution.py
@@ -30,17 +30,17 @@
 
 
 def block_kernel(
-    q_ref, k_ref, v_ref, x_ref, win_ref, pw_ref, gain_ref, up_ref, wq_hbm, wk_hbm, wv_hbm, wo_hbm,
+    q_hbm, k_hbm, v_hbm, x_hbm, win_ref, pw_ref, gain_ref, up_ref, wq_hbm, wk_hbm, wv_hbm, wo_hbm,
     out_hbm,
-    kbuf, vbuf, dist, stream, pooled_v, a_own, a_full, rs_all, ssq,
+    q_ref, x_ref, kbuf, vbuf, dist, stream, pooled_v, a_own, a_full, rs_all, ssq,
     w_all, wo_all, kv_part, q_part, kv_got, q_got, kv_all, q_all, top, total, mixed, h_all,
     keep, s_send, s_got, y_send, y_got, ring_sum, z_send, z_got, shifted, last_send, last_got,
-    hs_sem, hr_sem, azs_sem, azr_sem, ays_sem, ayr_sem, acs_sem, rss_sem, rsr_sem,
+    in_sem, hs_sem, hr_sem, azs_sem, azr_sem, ays_sem, ayr_sem, acs_sem, rss_sem, rsr_sem,
     ho_sem, wgs_sem, wgr_sem, ps_sem, pr_sem, kvs_sem, kvr_sem, hzs_sem, hzr_sem,
     ss_sem, sr_sem, ys_sem, yr_sem, zs_sem, zr_sem, l_sem, o_sem,
 ):
     rows, width = q_ref.shape
-    kv_width = k_ref.shape[1]
+    kv_width = kbuf.shape[1]
     reach = WIN // rows
     span = (reach + 1) * rows
     group = width // kv_width
@@ -96,6 +96,15 @@
             device_id=device, device_id_type=MESH,
         )
 
+    last_rows = pl.ds(reach * rows, rows)
+    loads = [
+        pltpu.make_async_copy(src, dst, in_sem.at[i])
+        for i, (src, dst) in enumerate(
+            ((k_hbm, kbuf.at[last_rows]), (v_hbm, vbuf.at[last_rows]), (q_hbm, q_ref), (x_hbm, x_ref))
+        )
+    ]
+    for load in loads:
+        load.start()
     barrier = pltpu.get_barrier_semaphore()
 
     def greet(device):
@@ -134,8 +143,8 @@
     def halo_near(which, hc, e):
         return halo_copy(which, hc, e, y_dev(e), jnp.where(y + e < RING, reach, 0))
 
-    kbuf[reach * rows :, :] = k_ref[...]
-    vbuf[reach * rows :, :] = v_ref[...]
+    loads[0].wait()
+    loads[1].wait()
     for hc in range(CHUNKS):
         for which in range(2):
             halo_far(which, hc).start()
@@ -245,8 +254,6 @@
 
         lax.fori_loop(0, SLOTS, one, 0)
 
-    origin(0)
-
     for hc in range(CHUNKS):
         for which in range(2):
             halo_far(which, hc).wait_recv()
@@ -257,6 +264,7 @@
                 def _():
                     halo_near(which, hc, e).start()
 
+    origin(0)
     q_at = lax.broadcasted_iota(jnp.int32, (rows, span), 0)
     l_at = lax.broadcasted_iota(jnp.int32, (rows, span), 1)
     gap = reach * rows + q_at - l_at
@@ -364,21 +372,14 @@
                     :, lanes(hc * q_chunk + p * piece_cols, piece_cols)
                 ]
 
-        @pl.when(hc == 1)
-        def _():
-            relay(0)
-            origin(1)
-
         @pl.when(hc == 2)
         def _():
             a_relay(0)
 
-        @pl.when(hc == 3)
-        def _():
-            relay(1)
-
-        return carry
-
+        return carry
+
+    loads[2].wait()
+    loads[3].wait()
     lax.fori_loop(0, CHUNKS, chunk, 0)
 
     mean = ssq[...].sum(-1, keepdims=True) * (1.0 / width)
@@ -401,6 +402,8 @@
         rs_copy(e, other).start()
 
     a_relay(1)
+    relay(0)
+    origin(1)
     for j in range(2):
         for e in range(1, RING):
             a_onward(j, e).wait_recv()
@@ -453,6 +456,7 @@
 
     project(0)
     project(1)
+    relay(1)
     row_scale = jnp.concatenate([rs_all[s] for s in range(n_tp)], axis=0)[:, 0:1]
     kv_all[mine] = (part_sum(0) * row_scale).astype(BF16)
 
@@ -479,10 +483,11 @@
     for h in range(heads):
         q_all[h] = q_rows[:, h * HEAD : (h + 1) * HEAD]
 
-    def attend(b, first):
+    def attend(b, first, some):
         keys = jnp.concatenate([kv_all[2 * b, :, :HEAD], kv_all[2 * b + 1, :, :HEAD]], axis=0)
         values = jnp.concatenate([kv_all[2 * b, :, HEAD:], kv_all[2 * b + 1, :, HEAD:]], axis=0)
-        for h in range(heads):
+        for u in range(2):
+            h = some * 2 + u
             s = lax.dot_general(
                 q_all[h], keys, (((1,), (1,)), ((), ())), preferred_element_type=F32
             ) * (LOG2E * HEAD**-0.5)
@@ -511,31 +516,49 @@
                 )
             top[h] = new_top
 
+    def h_piece(some, source):
+        return h_all.at[source, :, lanes(some * 2 * HEAD, 2 * HEAD)]
+
+    def h_copy(some, e):
+        return remote(
+            h_piece(some, z), h_piece(some, z), hzs_sem.at[some, e], hzr_sem.at[some, z], z_dev(e)
+        )
+
+    def h_arrival(some, e):
+        source = turn(z, e)
+        return remote(
+            h_piece(some, source), h_piece(some, source),
+            hzs_sem.at[some, e], hzr_sem.at[some, source], z_dev(e),
+        )
+
     kv_arrival(partner).wait_recv()
-    attend(pair, True)
-
-    def earlier(b, carry):
-        kv_arrival(2 * b).wait_recv()
-        kv_arrival(2 * b + 1).wait_recv()
-        attend(b, False)
-        return carry
-
-    lax.fori_loop(0, pair, earlier, 0)
-    for h in range(heads):
-        h_all[z, :, h * HEAD : (h + 1) * HEAD] = (mixed[h] / total[h]).astype(BF16)
-
-    def h_copy(e):
-        return remote(h_all.at[z], h_all.at[z], hzs_sem.at[e], hzr_sem.at[z], z_dev(e))
-
-    def h_arrival(e):
-        source = turn(z, e)
-        return remote(h_all.at[source], h_all.at[source], hzs_sem.at[e], hzr_sem.at[source], z_dev(e))
-
-    for e in range(1, RING):
-        h_copy(e).start()
+
+    def some_heads(some, carry):
+        attend(pair, True, some)
+
+        def earlier(b, carry):
+            @pl.when(some == 0)
+            def _():
+                kv_arrival(2 * b).wait_recv()
+                kv_arrival(2 * b + 1).wait_recv()
+
+            attend(b, False, some)
+            return carry
+
+        lax.fori_loop(0, pair, earlier, 0)
+        for u in range(2):
+            h = some * 2 + u
+            h_all[z, :, lanes(h * HEAD, HEAD)] = (mixed[h] / total[h]).astype(BF16)
+        for e in range(1, RING):
+            h_copy(some, e).start()
+        return carry
+
+    lax.fori_loop(0, heads // 2, some_heads, 0)
+
     finish(1)
-    for e in range(1, RING):
-        h_arrival(e).wait_recv()
+    for some in range(heads // 2):
+        for e in range(1, RING):
+            h_arrival(some, e).wait_recv()
 
     cols_out = wo_all.shape[2]
 
@@ -623,43 +646,51 @@
 
     lax.fori_loop(0, SLOTS, reduce_ring, 0)
 
-    def take_home(g, carry):
-        for e in range(1, RING):
-            z_arrival(g, e).wait_recv()
-            source = turn(z, e)
-            pooled_v[:, full_cols(g, source)] += z_got[a_rows(source), out_cols(g)].astype(F32)
-        return carry
-
-    lax.fori_loop(0, SLOTS, take_home, 0)
-
-    piece = last_send.shape[1]
-    for i in range(last_send.shape[0]):
-        last_send[i : i + 1, :] = pooled_v[own - 1 : own, i * piece : (i + 1) * piece]
-    last = remote(last_send, last_got, l_sem.at[0], l_sem.at[1], along(1))
-    last.start()
-    shifted[1:own, :] = pooled_v[0 : own - 1, :]
-    last.wait()
-    first_row = jnp.where(me == 0, 0.0, last_got[...])
-    for i in range(last_send.shape[0]):
-        shifted[0:1, i * piece : (i + 1) * piece] = first_row[i : i + 1, :]
+    def last(g):
+        return remote(
+            last_send.at[g], last_got.at[g], l_sem.at[0, g], l_sem.at[1, g], along(1)
+        )
 
     def result(h):
         return pltpu.make_async_copy(
             stream.at[h], out_hbm.at[:, lanes(h * HEAD, HEAD)], o_sem.at[h]
         )
 
-    def combine(i, carry):
-        for u in range(group):
-            h = i * group + u
-            cols = lanes(h * HEAD, HEAD)
-            add = shifted[:, cols]
-            for j in range(POOL):
-                where = pl.ds(j, own, stride=POOL)
-                stream[h, where, :] = stream[h, where, :] + up_ref[j : j + 1, cols] * add
-            result(h).start()
-        return carry
-
-    lax.fori_loop(0, width // HEAD // group, combine, 0)
+    def combine(g):
+        last(g).wait_recv()
+        for zz in range(RING):
+            where = full_cols(g, zz)
+            shifted[1:own, where] = pooled_v[0 : own - 1, where]
+            shifted[0:1, where] = jnp.where(me == 0, 0.0, last_got[g, zz : zz + 1, :])
+            for u in range(cols_out // HEAD):
+                h = ((g // 2) * n_tp + zz * 2 + lax.rem(g, 2)) * (cols_out // HEAD) + u
+                cols = lanes(h * HEAD, HEAD)
+                add = shifted[:, cols]
+                for j in range(POOL):
+                    rows_j = pl.ds(j, own, stride=POOL)
+                    stream[h, rows_j, :] = stream[h, rows_j, :] + up_ref[j : j + 1, cols] * add
+                result(h).start()
+
+    last_send[...] = jnp.zeros_like(last_send)
+
+    def take_home(g, carry):
+        @pl.when(g < SLOTS)
+        def _():
+            for e in range(1, RING):
+                z_arrival(g, e).wait_recv()
+                source = turn(z, e)
+                pooled_v[:, full_cols(g, source)] += z_got[a_rows(source), out_cols(g)].astype(F32)
+            for zz in range(RING):
+                last_send[g, zz : zz + 1, :] = pooled_v[own - 1 : own, full_cols(g, zz)]
+            last(g).start()
+
+        @pl.when(g > 0)
+        def _():
+            combine(g - 1)
+
+        return carry
+
+    lax.fori_loop(0, SLOTS + 1, take_home, 0)
 
     for hc in range(CHUNKS):
         for which in range(2):
@@ -693,7 +724,8 @@
     for e in range(1, RING):
         part_copy(0, e).wait_send()
         part_copy(1, e).wait_send()
-        h_copy(e).wait_send()
+        for some in range(heads // 2):
+            h_copy(some, e).wait_send()
     for e, other in others:
         rs_copy(e, other).wait_send()
 
@@ -709,6 +741,7 @@
         for e in range(1, RING):
             y_copy(g, e).wait_send()
             z_copy(g, e).wait_send()
+        last(g).wait_send()
         return carry
 
     lax.fori_loop(0, SLOTS, sums_settle, 0)
@@ -737,12 +770,14 @@
     return pl.pallas_call(
         block_kernel,
         out_shape=jax.ShapeDtypeStruct((rows, width), F32),
-        in_specs=[VMEM_SPEC] * 4
+        in_specs=[ANY_SPEC] * 4
         + [pl.BlockSpec(memory_space=pltpu.SMEM)]
         + [VMEM_SPEC] * 3
         + [ANY_SPEC] * 4,
         out_specs=ANY_SPEC,
         scratch_shapes=[
+            pltpu.VMEM((rows, width), BF16),
+            pltpu.VMEM((rows, width), BF16),
             pltpu.VMEM((span, kv_width), BF16),
             pltpu.VMEM((span, kv_width), BF16),
             pltpu.VMEM((rows, span), jnp.int32),
@@ -771,8 +806,9 @@
             pltpu.VMEM((RING * own, width // RING), BF16),
             pltpu.VMEM((RING * own, width // RING), BF16),
             pltpu.VMEM((own, width), F32),
-            pltpu.VMEM((8, width // 8), F32),
-            pltpu.VMEM((8, width // 8), F32),
+            pltpu.VMEM((SLOTS, 8, w_out.shape[1]), F32),
+            pltpu.VMEM((SLOTS, 8, w_out.shape[1]), F32),
+            dma((4,)),
             dma((2, CHUNKS, reach)),
             dma((2, CHUNKS, reach)),
             dma((CHUNKS, 2)),
@@ -789,15 +825,15 @@
             dma((2, RING)),
             dma((n_ctx,)),
             dma((n_ctx,)),
-            dma((RING,)),
-            dma((RING,)),
+            dma((heads // 2, RING)),
+            dma((heads // 2, RING)),
             dma((SLOTS,)),
             dma((SLOTS,)),
             dma((SLOTS, RING)),
             dma((SLOTS, RING)),
             dma((SLOTS, RING)),
             dma((SLOTS, RING)),
-            dma((2,)),
+            dma((2, SLOTS)),
             dma((width // HEAD,)),
         ],
         compiler_params=pltpu.CompilerParams(

time: 189 us -> 175 us (0.926)
  Pallas kernels: 183 us -> 167 us
    pallas_call x1, Pallas kernels: 183 us -> 167 us  [per_device(): pl.pallas_call(block_kernel, out_shape=jax.ShapeDtypeStruct((rows, width)...]
where the time goes in v4:
time: 175 us; the launch traced here: 172 us
  Pallas kernels  167 us (95%)
  local copies, waits for them, and re-layouts  4.61 us (3%)
    pallas_call x1, Pallas kernels, per_device(): pl.pallas_call(block_kernel, out_shape=jax.ShapeDtypeStruct((rows, width)...  167 us
    unnamed x1, local copies, waits for them, and re-layouts  4.61 us

profile of v4, /device:TPU:0, one launch (start us, length us, event | category | flops | bytes accessed | tf_op | source)
XLA Modules:
  0.0 171.8 jit_solution(4875985704659077250)
XLA Ops:
  0.0 167.2 %hourglass.1 = f32[128,8192]{1,0:T(8,128)} custom-call(bf16[128,8192]{1,0:T(8,128)(2,1)} %q_hbm.1, bf16[128,1024]{1,0:T(8,128)(2,1)} %k_hbm.1, bf16[128,1024]{1,0:T(8,128)(2,1)} %v_hbm.1, bf16[128,8192]{1,0:T(8,128)(2,1)} %x_hbm.1, s32[64]{0:T(128)} %win_ref.1, f32[4,8192]{1,0:T(4,128)} %pw_ref.1, f32[1,8192]{1,0:T(1,128)} %bitcast.1, f32[4,8192]{1,0:T(4,128)} %up_ref.1, ...), custom_call_target="tpu_custom_call" | custom-call | tf_op jit(solution)/shard_map/hourglass/pallas_call | solution.py:770
  167.2 4.6 %copy.14 = f32[128,8192]{1,0:T(8,128)} copy(f32[128,8192]{1,0:T(8,128)} %hourglass.1) | data formatting | bytes 8388608

commit v5 on v4

--- a/solution.py
+++ b/solution.py
@@ -33,10 +33,10 @@
     q_hbm, k_hbm, v_hbm, x_hbm, win_ref, pw_ref, gain_ref, up_ref, wq_hbm, wk_hbm, wv_hbm, wo_hbm,
     out_hbm,
     q_ref, x_ref, kbuf, vbuf, dist, stream, pooled_v, a_own, a_full, rs_all, ssq,
-    w_all, wo_all, kv_part, q_part, kv_got, q_got, kv_all, q_all, top, total, mixed, h_all,
+    w_all, wo_all, part, part_got, kv_all, q_all, top, total, mixed, h_all,
     keep, s_send, s_got, y_send, y_got, ring_sum, z_send, z_got, shifted, last_send, last_got,
-    in_sem, hs_sem, hr_sem, azs_sem, azr_sem, ays_sem, ayr_sem, acs_sem, rss_sem, rsr_sem,
-    ho_sem, wgs_sem, wgr_sem, ps_sem, pr_sem, kvs_sem, kvr_sem, hzs_sem, hzr_sem,
+    in_sem, hs_sem, hr_sem, azs_sem, azr_sem, ays_sem, ayr_sem, acs_sem, aps_sem, apr_sem, rss_sem, rsr_sem,
+    ho_sem, wgs_sem, wgr_sem, ps_sem, pr_sem, k1s_sem, k2s_sem, v1s_sem, v2s_sem, kr_sem, vr_sem, hzs_sem, hzr_sem,
     ss_sem, sr_sem, ys_sem, yr_sem, zs_sem, zr_sem, l_sem, o_sem,
 ):
     rows, width = q_ref.shape
@@ -145,7 +145,7 @@
 
     loads[0].wait()
     loads[1].wait()
-    for hc in range(CHUNKS):
+    for hc in range(2):
         for which in range(2):
             halo_far(which, hc).start()
 
@@ -183,7 +183,7 @@
         for i in range(4):
             hand_over(i).start()
 
-    for hc in range(CHUNKS):
+    for hc in range(2):
         for which in range(2):
             for e in range(1, RING):
 
@@ -254,9 +254,10 @@
 
         lax.fori_loop(0, SLOTS, one, 0)
 
-    for hc in range(CHUNKS):
+    for hc in range(2):
         for which in range(2):
             halo_far(which, hc).wait_recv()
+            halo_far(which, hc + 2).start()
         for which in range(2):
             for e in range(1, RING):
 
@@ -313,8 +314,26 @@
     def a_relay(j):
         for e in range(1, RING):
             a_z_arrival(j, e).wait_recv()
-        for e in range(RING):
+        for e in (1, 3, 0):
             a_copy(j, e).start()
+
+    def a_pass(j, side):
+        s = core * RING + turn(y, -1 if side == 0 else 1)
+        part_rows = block_rows // 2
+        piece = a_full.at[
+            sublanes((2 * s + side) * part_rows, part_rows), lanes(j * piece_cols, piece_cols)
+        ]
+        return remote(
+            piece, piece, aps_sem.at[j, side], apr_sem.at[j, side], y_dev(1 if side == 0 else -1)
+        )
+
+    def a_passed(j, side):
+        s = core * RING + turn(y, 2)
+        part_rows = block_rows // 2
+        piece = a_full.at[
+            sublanes((2 * s + side) * part_rows, part_rows), lanes(j * piece_cols, piece_cols)
+        ]
+        return remote(piece, piece, aps_sem.at[j, side], apr_sem.at[j, side], y_dev(2))
 
     part_heads = group // 2
 
@@ -322,6 +341,14 @@
         for which in range(2):
             for e in range(1, RING):
                 halo_near(which, hc, e).wait_recv()
+
+        @pl.when(hc < CHUNKS - 2)
+        def _():
+            for which in range(2):
+                halo_far(which, hc + 2).wait_recv()
+                for e in range(1, RING):
+                    halo_near(which, hc + 2, e).start()
+
         for u in range(kv_chunk // HEAD):
             kv_cols = lanes(hc * kv_chunk + u * HEAD, HEAD)
             keys = kbuf[:, kv_cols]
@@ -402,13 +429,19 @@
         rs_copy(e, other).start()
 
     a_relay(1)
-    relay(0)
+    for j in range(2):
+        for side, e in enumerate((1, 3)):
+            a_onward(j, e).wait_recv()
+            a_pass(j, side).start()
+            a_onward(j, e).start()
+        if j == 0:
+            relay(0)
+    for j in range(2):
+        a_passed(j, 0).wait_recv()
+        a_passed(j, 1).wait_recv()
+        a_onward(j, 2).start()
+    finish(0)
     origin(1)
-    for j in range(2):
-        for e in range(1, RING):
-            a_onward(j, e).wait_recv()
-            a_onward(j, e).start()
-    finish(0)
     for j in range(2):
         for y_at in range(RING):
             a_other(j, y_at).wait_recv()
@@ -416,21 +449,23 @@
         rs_arrival(e, other).wait_recv()
 
     def part_copy(kind, e):
-        part, got = ((kv_part, kv_got), (q_part, q_got))[kind]
-        return remote(
-            part.at[turn(z, e)], got.at[z], ps_sem.at[kind, e], pr_sem.at[kind, z], z_dev(e)
+        return remote(
+            part.at[kind, turn(z, e)], part_got.at[kind, z],
+            ps_sem.at[kind, e], pr_sem.at[kind, z], z_dev(e),
         )
 
     def part_arrival(kind, e):
-        part, got = ((kv_part, kv_got), (q_part, q_got))[kind]
         source = turn(z, e)
         return remote(
-            part.at[source], got.at[source], ps_sem.at[kind, e], pr_sem.at[kind, source], z_dev(e)
-        )
+            part.at[kind, source], part_got.at[kind, source],
+            ps_sem.at[kind, e], pr_sem.at[kind, source], z_dev(e),
+        )
+
+    two_heads = 2 * HEAD
 
     def project(kind):
-        part = (kv_part, q_part)[kind]
-        cols = (slice(q_width, None), slice(0, q_width))[kind]
+        first_col = (q_width, 0, two_heads)[kind]
+        cols = slice(first_col, first_col + two_heads)
 
         def one(m, carry):
             product = jnp.dot(
@@ -439,7 +474,7 @@
             for i in range(2):
                 for zz in range(RING):
                     first = (i * RING + zz) * own
-                    part[zz, a_rows(m * 2 + i), :] = product[first : first + own]
+                    part[kind, zz, a_rows(m * 2 + i), :] = product[first : first + own]
             return carry
 
         lax.fori_loop(0, RING, one, 0)
@@ -447,41 +482,105 @@
             part_copy(kind, e).start()
 
     def part_sum(kind):
-        part, got = ((kv_part, kv_got), (q_part, q_got))[kind]
-        value = part[z].astype(F32)
+        value = part[kind, z].astype(F32)
         for e in range(1, RING):
             part_arrival(kind, e).wait_recv()
-            value += got[turn(z, e)].astype(F32)
+            value += part_got[kind, turn(z, e)].astype(F32)
         return value
 
     project(0)
     project(1)
-    relay(1)
     row_scale = jnp.concatenate([rs_all[s] for s in range(n_tp)], axis=0)[:, 0:1]
     kv_all[mine] = (part_sum(0) * row_scale).astype(BF16)
 
-    def kv_copy(to):
-        return remote(
-            kv_all.at[mine], kv_all.at[mine], kvs_sem.at[to], kvr_sem.at[mine], group_dev(to)
-        )
-
-    def kv_arrival(source):
-        return remote(
-            kv_all.at[source], kv_all.at[source], kvs_sem.at[source], kvr_sem.at[source],
-            group_dev(source),
-        )
-
+    def home(x_at, z_at):
+        return (lax.rem(x_at, 2) * RING + z_at) * 2 + x_at // 2
+
+    def key_of(g):
+        return kv_all.at[g, :, 0:HEAD]
+
+    def value_of(g):
+        return kv_all.at[g, :, HEAD : 2 * HEAD]
+
+    def key_x(e):
+        to = turn(x, e)
+        copy = remote(key_of(mine), key_of(mine), k1s_sem.at[e], kr_sem.at[mine], at(to, z, y, core))
+        return copy, lax.rem(to, 2) >= x_lo
+
+    def key_z(x_at, e):
+        to, g, lo = turn(z, e), home(x_at, z), lax.rem(x_at, 2)
+        copy = remote(key_of(g), key_of(g), k2s_sem.at[x_at, e], kr_sem.at[g], at(x, to, y, core))
+        return copy, (lo < x_lo) | ((lo == x_lo) & (to > z))
+
+    def value_z(e):
+        to = turn(z, e)
+        copy = remote(
+            value_of(mine), value_of(mine), v1s_sem.at[e], vr_sem.at[mine], at(x, to, y, core)
+        )
+        return copy, (x_lo == 0) | (to > z)
+
+    def value_x(z_at, e):
+        to, g = turn(x, e), home(x, z_at)
+        lo = lax.rem(to, 2)
+        copy = remote(value_of(g), value_of(g), v2s_sem.at[z_at, e], vr_sem.at[g], at(to, z, y, core))
+        return copy, (lo > x_lo) | ((lo == x_lo) & (z_at <= z))
+
+    def key_arrival(g):
+        return remote(key_of(g), key_of(g), k1s_sem.at[0], kr_sem.at[g], sibling)
+
+    def value_arrival(g):
+        return remote(value_of(g), value_of(g), v1s_sem.at[0], vr_sem.at[g], sibling)
+
+    def begin(copy_and_wanted):
+        copy, wanted = copy_and_wanted
+
+        @pl.when(wanted)
+        def _():
+            copy.start()
+
+    def end(copy_and_wanted):
+        copy, wanted = copy_and_wanted
+
+        @pl.when(wanted)
+        def _():
+            copy.wait_send()
+
+    for e in range(1, RING):
+        begin(key_x(e))
+        begin(value_z(e))
+    for e in range(1, RING):
+        begin(value_x(z, e))
+        begin(key_z(x, e))
+
+    def kv_relay(e, carry):
+        x_at, z_at = turn(x, e), turn(z, e)
+
+        @pl.when(lax.rem(x_at, 2) <= x_lo)
+        def _():
+            key_arrival(home(x_at, z)).wait_recv()
+            for e2 in range(1, RING):
+                begin(key_z(x_at, e2))
+
+        @pl.when((x_lo == 0) | (z_at < z))
+        def _():
+            value_arrival(home(x, z_at)).wait_recv()
+            for e2 in range(1, RING):
+                begin(value_x(z_at, e2))
+
+        return carry
+
+    lax.fori_loop(1, RING, kv_relay, 0)
     partner = pair * 2 + 1 - x_hi
-
-    def kv_send(to, carry):
-        kv_copy(to).start()
-        return carry
-
-    kv_copy(partner).start()
-    lax.fori_loop(pair * 2 + 2, n_ctx, kv_send, 0)
-    q_rows = (part_sum(1) * row_scale).astype(BF16)
-    for h in range(heads):
-        q_all[h] = q_rows[:, h * HEAD : (h + 1) * HEAD]
+    project(2)
+    relay(1)
+
+    def take_queries(some):
+        scale = jnp.concatenate([rs_all[s] for s in range(n_tp)], axis=0)[:, 0:1]
+        q_rows = (part_sum(1 + some) * scale).astype(BF16)
+        for u in range(2):
+            q_all[some * 2 + u] = q_rows[:, u * HEAD : (u + 1) * HEAD]
+
+    take_queries(0)
 
     def attend(b, first, some):
         keys = jnp.concatenate([kv_all[2 * b, :, :HEAD], kv_all[2 * b + 1, :, :HEAD]], axis=0)
@@ -531,16 +630,28 @@
             hzs_sem.at[some, e], hzr_sem.at[some, source], z_dev(e),
         )
 
-    kv_arrival(partner).wait_recv()
+    value_arrival(partner).wait_recv()
 
     def some_heads(some, carry):
+        @pl.when(some == 1)
+        def _():
+            take_queries(1)
+
         attend(pair, True, some)
 
         def earlier(b, carry):
             @pl.when(some == 0)
             def _():
-                kv_arrival(2 * b).wait_recv()
-                kv_arrival(2 * b + 1).wait_recv()
+                @pl.when(lax.rem(b, RING) != z)
+                def _():
+                    key_arrival(2 * b).wait_recv()
+                    key_arrival(2 * b + 1).wait_recv()
+
+                for hi in range(2):
+
+                    @pl.when(2 * hi + b // RING != x)
+                    def _():
+                        value_arrival(2 * b + hi).wait_recv()
 
             attend(b, False, some)
             return carry
@@ -583,7 +694,6 @@
         s_copy(g).start()
         return carry
 
-    lax.fori_loop(0, SLOTS, multiply, 0)
 
     def y_rows(y_at):
         return sublanes(y_at * block_rows, block_rows)
@@ -612,7 +722,18 @@
         )
         return carry
 
-    lax.fori_loop(0, SLOTS, reduce_cores, 0)
+    def sums(g, carry):
+        @pl.when(g < SLOTS)
+        def _():
+            multiply(g, 0)
+
+        @pl.when(g > 0)
+        def _():
+            reduce_cores(g - 1, 0)
+
+        return carry
+
+    lax.fori_loop(0, SLOTS + 1, sums, 0)
 
     def z_copy(g, e):
         return remote(
@@ -717,24 +838,38 @@
 
     lax.fori_loop(0, CHUNKS, a_settle, 0)
     for j in range(2):
-        for e in range(RING):
+        for e in (1, 3, 0):
             a_copy(j, e).wait_send()
+        a_pass(j, 0).wait_send()
+        a_pass(j, 1).wait_send()
         for e in range(1, RING):
             a_onward(j, e).wait_send()
     for e in range(1, RING):
-        part_copy(0, e).wait_send()
-        part_copy(1, e).wait_send()
+        for kind in range(3):
+            part_copy(kind, e).wait_send()
         for some in range(heads // 2):
             h_copy(some, e).wait_send()
     for e, other in others:
         rs_copy(e, other).wait_send()
 
-    def kv_settle(to, carry):
-        kv_copy(to).wait_send()
-        return carry
-
-    kv_copy(partner).wait_send()
-    lax.fori_loop(pair * 2 + 2, n_ctx, kv_settle, 0)
+    for e in range(1, RING):
+        end(key_x(e))
+        end(value_z(e))
+
+    def kv_settle(i, carry):
+        for e in range(1, RING):
+
+            @pl.when(lax.rem(i, 2) <= x_lo)
+            def _():
+                end(key_z(i, e))
+
+            @pl.when((x_lo == 0) | (i <= z))
+            def _():
+                end(value_x(i, e))
+
+        return carry
+
+    lax.fori_loop(0, RING, kv_settle, 0)
 
     def sums_settle(g, carry):
         s_copy(g).wait_send()
@@ -789,10 +924,8 @@
             pltpu.VMEM((own, HEAD), F32),
             pltpu.VMEM((SLOTS * depth, w_cols), BF16),
             pltpu.VMEM((SLOTS,) + w_out.shape, BF16),
-            pltpu.VMEM((RING, all_rows, 2 * HEAD), BF16),
-            pltpu.VMEM((RING, all_rows, q_width), BF16),
-            pltpu.VMEM((RING, all_rows, 2 * HEAD), BF16),
-            pltpu.VMEM((RING, all_rows, q_width), BF16),
+            pltpu.VMEM((3, RING, all_rows, 2 * HEAD), BF16),
+            pltpu.VMEM((3, RING, all_rows, 2 * HEAD), BF16),
             pltpu.VMEM((n_ctx, all_rows, 2 * HEAD), BF16),
             pltpu.VMEM((heads, all_rows, HEAD), BF16),
             pltpu.VMEM((heads, all_rows, 1), F32),
@@ -816,13 +949,19 @@
             dma((2, RING)),
             dma((2, n_tp)),
             dma((2, RING)),
+            dma((2, 2)),
+            dma((2, 2)),
             dma((2, RING)),
             dma((n_tp,)),
             dma((3, 4)),
             dma((2, SLOTS, 2)),
             dma((2, SLOTS)),
-            dma((2, RING)),
-            dma((2, RING)),
+            dma((3, RING)),
+            dma((3, RING)),
+            dma((RING,)),
+            dma((RING, RING)),
+            dma((RING,)),
+            dma((RING, RING)),
             dma((n_ctx,)),
             dma((n_ctx,)),
             dma((heads // 2, RING)),

time: 175 us -> 160 us (0.914); the launches traced: 172 us -> 159 us
  Pallas kernels: 167 us -> 154 us
    pallas_call x1, Pallas kernels: 167 us -> 154 us  [per_device(): pl.pallas_call(block_kernel, out_shape=jax.ShapeDtypeStruct((rows, width)...]
where the time goes in v5:
time: 160 us; the launch traced here: 159 us
  Pallas kernels  154 us (96%)
  local copies, waits for them, and re-layouts  4.61 us (3%)
    pallas_call x1, Pallas kernels, per_device(): pl.pallas_call(block_kernel, out_shape=jax.ShapeDtypeStruct((rows, width)...  154 us
    unnamed x1, local copies, waits for them, and re-layouts  4.61 us

profile of v5, /device:TPU:0, one launch (start us, length us, event | category | flops | bytes accessed | tf_op | source)
XLA Modules:
  0.0 158.7 jit_solution(13124446205960311773)
XLA Ops:
  0.0 154.1 %hourglass.1 = f32[128,8192]{1,0:T(8,128)} custom-call(bf16[128,8192]{1,0:T(8,128)(2,1)} %q_hbm.1, bf16[128,1024]{1,0:T(8,128)(2,1)} %k_hbm.1, bf16[128,1024]{1,0:T(8,128)(2,1)} %v_hbm.1, bf16[128,8192]{1,0:T(8,128)(2,1)} %x_hbm.1, s32[64]{0:T(128)} %win_ref.1, f32[4,8192]{1,0:T(4,128)} %pw_ref.1, f32[1,8192]{1,0:T(1,128)} %bitcast.1, f32[4,8192]{1,0:T(4,128)} %up_ref.1, ...), custom_call_target="tpu_custom_call" | custom-call | tf_op jit(solution)/shard_map/hourglass/pallas_call | solution.py:905
  154.1 4.6 %copy.14 = f32[128,8192]{1,0:T(8,128)} copy(f32[128,8192]{1,0:T(8,128)} %hourglass.1) | data formatting | bytes 8388608
